TPU v7x, 512 devices: a whole 4x4x16 slice. The times are simulated.
512 devices in a mesh: dp: 4 (over y), seq: 16 (over z), expert: 8 (over x, core).
Axes of the slice: x: 4, y: 4, z: 16, core: 2. Of those that a mesh axis runs over, the one named last changes fastest.
Arguments:
- moe_cotangent: bfloat16 [4096, 4096], P(('dp', 'seq', 'expert')), may hold values from -6 to 6
- route_ids: int32 [4096, 2], P(('dp', 'seq', 'expert')), may hold values from 0 to 7, all different within a row; in each aligned block of 8 rows (0 to 7, 8 to 15, ...) at most 2 rows name the same one
- route_weights: bfloat16 [4096, 2], P(('dp', 'seq', 'expert')), may hold values from 0.099609375 to 0.8984375
- saved_pre: bfloat16 [8, 1024, 12288], P('expert', None, ('dp', 'seq')), may hold values from -24 to 24
- w_down: bfloat16 [8, 12288, 4096], P('expert', ('dp', 'seq')), may hold values from -0.0546875 to 0.0546875
- inputs: bfloat16 [4096, 8192], P('seq', ('dp', 'expert')), may hold values from -6 to 6
- deltas: bfloat16 [4096, 8192], P('seq', ('dp', 'expert')), may hold values from 0.25 to 2
- mamba_cotangent: bfloat16 [4096, 8192], P('seq', ('dp', 'expert')), may hold values from -6 to 6
- b_proj: float32 [4096, 16], P('seq'), may hold values from -6 to 6
- c_proj: float32 [4096, 16], P('seq'), may hold values from -6 to 6
- decay_rates: float32 [16, 8192], P(None, ('dp', 'expert')), may hold values from 2.4414063e-05 to 0.2
- skip_gain: float32 [8192], P(('dp', 'expert')), may hold values from 0.5 to 1.5
- documents: int32 [4096], P('seq'), may hold values from 0 to 3, as said below
Outputs:
- w_down_grad: bfloat16 [8, 12288, 4096], P('expert', ('dp', 'seq'))
- route_grad: float32 [4096, 2], P(('dp', 'seq', 'expert'))
- pre_grad: bfloat16 [8, 1024, 12288], P('expert', None, ('dp', 'seq'))
- input_grad: bfloat16 [4096, 8192], P('seq', ('dp', 'expert'))
- delta_grad: bfloat16 [4096, 8192], P('seq', ('dp', 'expert'))
- b_grad: float32 [4096, 16], P('seq')
- c_grad: float32 [4096, 16], P('seq')
- rate_grad: float32 [16, 8192], P(None, ('dp', 'expert'))
- skip_grad: float32 [8192], P(('dp', 'expert'))
Inputs may be any that keep to these rules, and one draw needn't show every extreme that they name: `route_ids`: in every aligned block of 8 rows (the rows of one device) no expert is named by more than 2 rows, a bound that some block reaches. `documents`: the numbers never fall, start at 0 and step by one; every document covers one token or more.
All inputs are finite; a program needn't handle non-finite values.
Results may differ from a plain program's by a relative error of at most 0.00225.
The roundings to bfloat16 on the way count: a program that leaves them out, or rounds other values in their place, can miss the bound.
Values may be sent and summed in bfloat16 or wider, within the bound.
A program may use at most 64 MiB of HBM per device.

v0:
```python
import math

import jax
import jax.numpy as jnp
from jax import lax
from jax.sharding import PartitionSpec as P


def shifted_2(value, axis, steps):
    count = lax.axis_size(axis)
    first, last = (max(0, -steps), min(count, count - steps))
    return lax.ppermute(value, axis, [(source, source + steps) for source in range(first, last)])


def prefix(value, axis, join, neutral, backward):
    count, mine = (lax.axis_size(axis), lax.axis_index(axis))
    pieces = jax.tree.map(lambda part: lax.all_gather(part, axis), value)
    if backward:
        pieces = jax.tree.map(lambda part: part[::-1], pieces)
        mine = count - 1 - mine
    total = jax.tree.map(
        lambda part, zero: jnp.full_like(part, 0) + jnp.asarray(zero, part.dtype), value, neutral
    )

    def step(position, total):
        longer = join(total, jax.tree.map(lambda part: part[position], pieces))
        return jax.tree.map(lambda new, old: jnp.where(position < mine, new, old), longer, total)

    return lax.fori_loop(0, count - 1, step, total)


def affine_pair(earlier, latter):
    return (latter[0] * earlier[0], latter[0] * earlier[1] + latter[1])


def silu_slope(preact):
    sigmoid = jax.nn.sigmoid(preact)
    return sigmoid * (1.0 + preact * (1.0 - sigmoid))


def slot_rows(route_block, experts, capacity):
    flat_ids = route_block.reshape(-1)
    onehot = (flat_ids[:, None] == jnp.arange(experts, dtype=jnp.int32)[None, :]).astype(jnp.int32)
    before = jnp.cumsum(onehot, axis=0, dtype=jnp.int32) - onehot
    position = jnp.sum(before * onehot, axis=1)
    return flat_ids * capacity + position


def decay_table(deltas32, rate_row, keep_mask):
    return jnp.exp(-deltas32 * rate_row[None, :]) * keep_mask[:, None]


def forward_local(decays, driving):
    return lax.associative_scan(affine_pair, (decays, driving), axis=0)


def backward_local(decays, source):
    shifted = jnp.concatenate([decays[1:], jnp.ones_like(decays[:1])], axis=0)
    return lax.associative_scan(affine_pair, (shifted, source), axis=0, reverse=True)


def block_summary(inputs32, deltas32, cot32, b_column, c_column, rate_row, keep_mask):
    decays = decay_table(deltas32, rate_row, keep_mask)
    cumulative, state_local = forward_local(decays, deltas32 * b_column[:, None] * inputs32)
    remaining, adjoint_local = backward_local(decays, c_column[:, None] * cot32)
    return (cumulative[-1], state_local[-1], decays[0] * adjoint_local[0])


def state_pass(
    inputs32, deltas32, cot32, b_column, c_column, rate_row, keep_mask, state_in, adjoint_in
):
    decays = decay_table(deltas32, rate_row, keep_mask)
    cumulative, state_local = forward_local(decays, deltas32 * b_column[:, None] * inputs32)
    remaining, adjoint_local = backward_local(decays, c_column[:, None] * cot32)
    states = state_local + cumulative * state_in[None, :]
    adjoint = adjoint_local + remaining * adjoint_in[None, :]
    previous = jnp.concatenate([state_in[None, :], states[:-1]], axis=0)
    carried = decays * previous
    input_part = deltas32 * b_column[:, None] * adjoint
    delta_part = adjoint * (b_column[:, None] * inputs32 - rate_row[None, :] * carried)
    b_part = jnp.sum(adjoint * deltas32 * inputs32, axis=1)
    c_part = jnp.sum(cot32 * states, axis=1)
    rate_part = -jnp.sum(adjoint * deltas32 * carried, axis=0)
    return (input_part, delta_part, b_part, c_part, rate_part)


def mamba_sweep(
    inputs32, deltas32, cot32, b_rows, c_rows, rates, keep_mask, states_in, adjoints_in
):

    def per_state(totals, state_items):
        rate_row, b_column, c_column, state_in, adjoint_in = state_items
        input_part, delta_part, b_part, c_part, rate_part = state_pass(
            inputs32, deltas32, cot32, b_column, c_column, rate_row, keep_mask, state_in, adjoint_in
        )
        return ((totals[0] + input_part, totals[1] + delta_part), (b_part, c_part, rate_part))

    blank = jnp.zeros_like(inputs32)
    sums, columns = lax.scan(
        per_state, (blank, blank), (rates, b_rows.T, c_rows.T, states_in, adjoints_in)
    )
    return (sums[0], sums[1], columns[0].T, columns[1].T, columns[2])


def route_terms(rows_piece, hidden_piece, weight_here):
    count = rows_piece.shape[0]
    width = math.gcd(count, 512)

    def one_block(packed):
        rows_block, hidden_block = packed
        produced = jnp.dot(hidden_block, weight_here, preferred_element_type=jnp.float32)
        return jnp.sum(rows_block.astype(jnp.float32) * produced, axis=1)

    sums = lax.map(
        one_block,
        (
            rows_piece.reshape(count // width, width, rows_piece.shape[1]),
            hidden_piece.reshape(count // width, width, hidden_piece.shape[1]),
        ),
    )
    return sums.reshape(count)


def local(
    moe_cotangent,
    route_ids,
    route_weights,
    saved_pre,
    w_down,
    inputs,
    deltas,
    mamba_cotangent,
    b_proj,
    c_proj,
    decay_rates,
    skip_gain,
    documents,
):
    expert_count = lax.axis_size("expert")
    run_count = lax.axis_size("dp") * lax.axis_size("seq")
    tokens_here = moe_cotangent.shape[0]
    model_width = moe_cotangent.shape[1]
    rows_total = saved_pre.shape[1]
    run_rows = rows_total // run_count
    capacity = run_rows // expert_count
    choose = route_ids.shape[1]
    pair_count = tokens_here * choose
    target = slot_rows(route_ids, expert_count, capacity)
    matched = target[None, :] == jnp.arange(expert_count * capacity, dtype=jnp.int32)[:, None]
    filled = jnp.any(matched, axis=1)
    pair_index = jnp.sum(
        jnp.where(matched, jnp.arange(pair_count, dtype=jnp.int32)[None, :], 0), axis=1
    )
    token_index = pair_index // choose
    send_rows = jnp.where(filled[:, None], moe_cotangent[token_index], jnp.zeros((), jnp.bfloat16))
    send_scales = jnp.where(
        filled, route_weights.reshape(-1)[pair_index], jnp.zeros((), jnp.bfloat16)
    )
    received, scales = (
        lax.all_to_all(
            send_rows.reshape(expert_count, capacity, model_width),
            "expert",
            split_axis=0,
            concat_axis=0,
            tiled=True,
        ),
        lax.all_to_all(
            send_scales.reshape(expert_count, capacity),
            "expert",
            split_axis=0,
            concat_axis=0,
            tiled=True,
        ),
    )
    received = received.reshape(run_rows, model_width)
    scales = scales.reshape(run_rows)
    preact = saved_pre[0].astype(jnp.float32)
    hidden = jax.nn.silu(preact).astype(jnp.bfloat16)
    weight_here = w_down[0]
    all_rows, all_scales = (
        lax.all_gather(received, ("dp", "seq"), axis=0, tiled=True),
        lax.all_gather(scales, ("dp", "seq"), axis=0, tiled=True),
    )
    scale_column = all_scales.astype(jnp.float32)[:, None]
    scaled = (all_rows.astype(jnp.float32) * scale_column).astype(jnp.bfloat16)
    weight_sum = lax.dot_general(
        hidden, scaled, (((0,), (0,)), ((), ())), preferred_element_type=jnp.float32
    )
    back = lax.dot_general(
        all_rows, weight_here, (((1,), (1,)), ((), ())), preferred_element_type=jnp.float32
    )
    route_part = route_terms(all_rows, hidden, weight_here)
    hidden_grad = scale_column * back
    pre_grad = (hidden_grad * silu_slope(preact)).astype(jnp.bfloat16)[None]
    w_down_grad = weight_sum.astype(jnp.bfloat16)[None]
    route_mine = lax.psum_scatter(route_part, ("dp", "seq"), scatter_dimension=0, tiled=True)
    returned = lax.all_to_all(
        route_mine.reshape(expert_count, capacity),
        "expert",
        split_axis=0,
        concat_axis=0,
        tiled=True,
    )
    route_grad = returned.reshape(-1)[target].reshape(tokens_here, choose)
    inputs32 = inputs.astype(jnp.float32)
    deltas32 = deltas.astype(jnp.float32)
    cot32 = mamba_cotangent.astype(jnp.float32)
    prior = shifted_2(documents[-1:], "seq", 1)
    earlier_docs = jnp.concatenate([prior, documents[:-1]])
    keep_mask = (documents == earlier_docs).astype(jnp.float32)
    through, state_last, adjoint_first = lax.map(
        lambda packed: block_summary(
            inputs32, deltas32, cot32, packed[1], packed[2], packed[0], keep_mask
        ),
        (decay_rates, b_proj.T, c_proj.T),
    )
    identity = (jnp.ones_like(through), jnp.zeros_like(through))
    state_in = prefix((through, state_last), "seq", affine_pair, identity, False)[1]
    adjoint_in = prefix((through, adjoint_first), "seq", affine_pair, identity, True)[1]
    input_sum, delta_sum, b_part, c_part, rate_rows = mamba_sweep(
        inputs32, deltas32, cot32, b_proj, c_proj, decay_rates, keep_mask, state_in, adjoint_in
    )
    input_grad = (input_sum + skip_gain[None, :] * cot32).astype(jnp.bfloat16)
    delta_grad = delta_sum.astype(jnp.bfloat16)
    skip_local = jnp.sum(cot32 * inputs32, axis=0)
    b_grad, c_grad = lax.psum((b_part, c_part), ("dp", "expert"))
    rate_grad, skip_grad = lax.psum((rate_rows, skip_local), "seq")
    return (
        w_down_grad,
        route_grad,
        pre_grad,
        input_grad,
        delta_grad,
        b_grad,
        c_grad,
        rate_grad,
        skip_grad,
    )


def solution(mesh):
    return jax.shard_map(
        local,
        mesh=mesh,
        in_specs=(
            P(("dp", "seq", "expert"), None),
            P(("dp", "seq", "expert"), None),
            P(("dp", "seq", "expert"), None),
            P("expert", None, ("dp", "seq")),
            P("expert", ("dp", "seq"), None),
            P("seq", ("dp", "expert")),
            P("seq", ("dp", "expert")),
            P("seq", ("dp", "expert")),
            P("seq", None),
            P("seq", None),
            P(None, ("dp", "expert")),
            P(("dp", "expert")),
            P("seq"),
        ),
        out_specs=(
            P("expert", ("dp", "seq"), None),
            P(("dp", "seq", "expert"), None),
            P("expert", None, ("dp", "seq")),
            P("seq", ("dp", "expert")),
            P("seq", ("dp", "expert")),
            P("seq", None),
            P("seq", None),
            P(None, ("dp", "expert")),
            P(("dp", "expert")),
        ),
        check_vma=False,
    )
```

profile of v0, /device:TPU:1, one launch (start us, length us, event | category | flops | bytes accessed | tf_op | source)
XLA Modules:
  0.0 1068.3 jit_solution(4920929993474398655)
XLA Ops:
  10.3 10.2 all-to-all-start
  21.7 1.8 collective-permute-start
  33.2 1.4 fusion.87
  35.9 2.0 compare_convert_fusion
  37.9 129.3 %while.74 = (s32[]{:T(128)}, f32[16,256]{1,0:T(8,128)S(1)}, f32[16,256]{1,0:T(8,128)S(1)}, f32[16,256]{1,0:T(8,128)S(1)}, f32[16,256]{1,0:T(8,128)}, /*index=5*/...) while((s32[]{:T(128)}, f32[16,256]{1,0:T(8,128)S(1)}, ...), condition=%wide.region_9.10_spmd, body=%wide.region_8.9_spmd.sunk | while | flops 1256962 | bytes 20462932 | solution.py:211
  167.1 25.4 %all-gather = f32[256,256]{1,0:T(8,128)S(1)} all-gather(f32[16,256]{1,0:T(8,128)S(1)} %get-tuple-element.479), channel_id=2, replica_groups=mesh['dp'=4,'seq'=16,'expert'=8] {'seq'}, dimensions={0}, use_global_device_ids=true | all-gather | bytes 278528 | tf_op jit(solution)/shard_map/all_gather | solution.py:17
  192.5 21.3 %all-gather.1 = f32[256,256]{1,0:T(8,128)S(1)} all-gather(f32[16,256]{1,0:T(8,128)S(1)} %get-tuple-element.480), channel_id=3, replica_groups=mesh['dp'=4,'seq'=16,'expert'=8] {'seq'}, dimensions={0}, use_global_device_ids=true | all-gather | bytes 278528 | tf_op jit(solution)/shard_map/all_gather | solution.py:17
  213.8 19.3 %while.75 = (s32[]{:T(128)}, f32[16,256]{1,0:T(8,128)}, s32[]{:T(128)}, f32[16,16,256]{2,1,0:T(8,128)S(1)}, f32[16,16,256]{2,1,0:T(8,128)S(1)}, /*index=5*/s32[]{:T(128)}, s32[]{:T(128)}) while((s32[]{:T(128)}, f32[16,256]{1,0:T(8,128)}, s32[]{:T(128)}, f32[16,16,256]{2,1,0:T(8,128)S(1)}, f32[16,16,256]{2,1,0:T(8,128)S(1)}, ...), condition=%wide.region_13.14_spmd.clone, body=%wide.region_12.13_spmd.clone.sunk | while | flops 16388 | bytes 65645 | solution.py:29
  214.4 1.3 fusion.151
  215.8 1.3 fusion.151
  217.1 1.3 fusion.151
  218.4 1.3 fusion.151
  219.8 1.3 fusion.151
  221.1 1.3 fusion.151
  222.4 1.3 fusion.151
  225.1 1.3 fusion.151
  229.1 1.3 fusion.151
  233.1 22.6 %all-gather.2 = f32[256,256]{1,0:T(8,128)S(1)} all-gather(f32[16,256]{1,0:T(8,128)S(1)} %get-tuple-element.482), channel_id=4, replica_groups=mesh['dp'=4,'seq'=16,'expert'=8] {'seq'}, dimensions={0}, use_global_device_ids=true | all-gather | bytes 278528 | tf_op jit(solution)/shard_map/all_gather | solution.py:17
  256.2 26.0 %all-to-all-start.1 = ((bf16[8,1,2]{2,1,0:T(2,128)(2,1)}), bf16[8,1,2]{2,1,0:T(2,128)(2,1)}, u32[]{:S(2)}, u32[]{:S(2)}) async-start(bf16[8,1,2]{2,1,0:T(2,128)(2,1)} %select_n.120), calls=%async_computation.1 | async-start | bytes 8192 | tf_op jit(solution)/shard_map/all_to_all | solution.py:167
  284.8 284.3 %while.77 = (s32[]{:T(128)}, f32[256,256]{1,0:T(8,128)S(1)}, f32[256,256]{1,0:T(8,128)}, f32[16,256]{1,0:T(8,128)}, f32[16,256]{1,0:T(8,128)}, /*index=5*/f32[16...) while((s32[]{:T(128)}, f32[256,256]{1,0:T(8,128)S(1)}, ...), condition=%wide.region_18.19_spmd.clone, body=%wide.region_14.18_spmd.clone.sunk | while | flops 3739139 | bytes 39566932 | solution.py:99
  298.5 1.4 dynamic_update_slice.43
  316.3 1.4 dynamic_update_slice.43
  334.1 1.4 dynamic_update_slice.43
  351.8 1.4 dynamic_update_slice.43
  369.6 1.4 dynamic_update_slice.43
  387.4 1.4 dynamic_update_slice.43
  405.1 1.4 dynamic_update_slice.43
  422.9 1.4 dynamic_update_slice.43
  440.7 1.4 dynamic_update_slice.43
  458.5 1.4 dynamic_update_slice.43
  476.2 1.4 dynamic_update_slice.43
  494.0 1.4 dynamic_update_slice.43
  511.8 1.4 dynamic_update_slice.43
  529.5 1.4 dynamic_update_slice.43
  547.3 1.4 dynamic_update_slice.43
  565.0 1.4 dynamic_update_slice.43
  569.0 1.6 convert_element_type.77
  570.6 123.6 %all-reduce.117 = (f32[256,16]{0,1:T(8,128)}, f32[256,16]{0,1:T(8,128)}) all-reduce(f32[256,16]{0,1:T(8,128)} %bitcast.163, f32[256,16]{0,1:T(8,128)} %bitcast.164), channel_id=1, replica_groups=mesh['dp'=4,'seq'=16,'expert'=8] {'dp','expert'}, use_global_device_ids=true, to_apply=%region_19.20 | all-reduce | flops 8192 | bytes 65536 | tf_op jit(solution)/shard_map/psum | solution.py:226
  694.2 1.7 multiply_reduce_fusion.3
  695.9 39.0 %all-reduce.118 = (f32[16,256]{1,0:T(8,128)}, f32[256]{0:T(256)}) all-reduce(f32[16,256]{1,0:T(8,128)} %get-tuple-element.488, f32[256]{0:T(256)S(1)} %get-tuple-element.832), channel_id=1, replica_groups=mesh['dp'=4,'seq'=16,'expert'=8] {'seq'}, use_global_device_ids=true, to_apply=%region_21.22 | all-reduce | flops 4352 | bytes 34816 | tf_op jit(solution)/shard_map/psum | solution.py:227
  735.9 111.5 %all-reduce.115 = bf16[1024]{0:T(1024)(128)(2,1)S(1)} all-reduce(bf16[1024]{0:T(1024)(128)(2,1)S(1)} %dynamic-update-slice), channel_id=1, replica_groups=mesh['dp'=4,'seq'=16,'expert'=8] {'dp','seq'}, use_global_device_ids=true, to_apply=%add.115 | all-reduce | flops 1024 | bytes 4096
  847.5 9.5 while.73
  847.5 4.1 fusion.132
  852.3 4.1 fusion.132
  857.7 111.7 %all-reduce.116 = f32[1024]{0:T(1024)S(1)} all-reduce(f32[1024]{0:T(1024)S(1)} %bitcast.166), channel_id=5, replica_groups=mesh['dp'=4,'seq'=16,'expert'=8] {'dp','seq'}, use_global_device_ids=true, to_apply=%region_7.8.clone | all-reduce | flops 1024 | bytes 8192
  970.1 77.5 %all-to-all-start.2 = ((f32[8,1,2]{2,1,0:T(1,128)}), f32[8,1,2]{2,1,0:T(1,128)S(1)}, u32[]{:S(2)}, u32[]{:S(2)}) async-start(f32[8,1,2]{2,1,0:T(1,128)} %bitcast.14), calls=%async_computation.2 | async-start | bytes 8192 | tf_op jit(solution)/shard_map/all_to_all | solution.py:197
  1047.6 7.7 fusion.51
  1055.3 3.4 fusion.48
  (7976 shorter events, 383.0 us)
Async XLA Ops:
  10.3 245.9 %all-to-all-start = ((bf16[8,2,4096]{2,1,0:T(2,128)(2,1)}), bf16[8,2,4096]{2,1,0:T(2,128)(2,1)S(1)}, u32[]{:S(2)}, u32[]{:S(2)}) async-start(bf16[8,2,4096]{2,1,0:T(2,128)(2,1)} %broadcast_select_fusion), calls=%async_computation | async-start | bytes 262144 | tf_op jit(solution)/shard_map/all_to_all | solution.py:160
  21.7 14.1 %collective-permute-start = (s32[1]{0:T(128)}, s32[1]{0:T(128)}, u32[]{:S(2)}, u32[]{:S(2)}) collective-permute-start(s32[1]{0:T(128)} %slice.1229), channel_id=1, source_target_pairs={{0,8},{8,16},{16,24},{24,32},{32,40},{40,48},{48,56},{56,64},{64,7... | collective-permute-start | bytes 20 | tf_op jit(solution)/shard_map/ppermute | solution.py:12
  256.2 478.7 %all-to-all-start.1 = ((bf16[8,1,2]{2,1,0:T(2,128)(2,1)}), bf16[8,1,2]{2,1,0:T(2,128)(2,1)}, u32[]{:S(2)}, u32[]{:S(2)}) async-start(bf16[8,1,2]{2,1,0:T(2,128)(2,1)} %select_n.120), calls=%async_computation.1 | async-start | bytes 8192 | tf_op jit(solution)/shard_map/all_to_all | solution.py:167
  282.2 565.3 %all-gather.5.cloned.1.call-start = ((), (), s32[]{:S(2)}) async-start(), calls=%async_computation.3 | async-start | bytes 8519680 | tf_op jit(solution)/shard_map/all_gather | solution.py:181
  288.3 5.2 copy-start.3
  293.6 4.0 copy-start.1
  306.0 5.2 copy-start.3
  311.4 4.0 copy-start.1
  323.8 5.2 copy-start.3
  329.2 4.0 copy-start.1
  341.6 5.2 copy-start.3
  346.9 4.0 copy-start.1
  359.3 5.2 copy-start.3
  364.7 4.0 copy-start.1
  369.6 4.0 copy-start.2
  377.1 5.2 copy-start.3
  382.5 4.0 copy-start.1
  387.4 4.0 copy-start.2
  394.9 5.2 copy-start.3
  400.3 4.0 copy-start.1
  412.6 5.2 copy-start.3
  418.0 4.0 copy-start.1
  422.9 4.0 copy-start.2
  430.4 5.2 copy-start.3
  435.8 4.0 copy-start.1
  440.7 4.0 copy-start.2
  448.2 5.2 copy-start.3
  453.6 4.0 copy-start.1
  458.4 4.0 copy-start.2
  465.9 5.2 copy-start.3
  471.3 4.0 copy-start.1
  476.2 4.0 copy-start.2
  483.7 5.2 copy-start.3
  489.1 4.0 copy-start.1
  494.0 4.0 copy-start.2
  501.5 5.2 copy-start.3
  506.9 4.0 copy-start.1
  519.2 5.2 copy-start.3
  524.6 4.0 copy-start.1
  537.0 5.2 copy-start.3
  542.4 4.0 copy-start.1
  554.8 5.2 copy-start.3
  560.1 4.0 copy-start.1
  847.5 200.1 %copy-start.4 = (bf16[1,1024,192]{1,2,0:T(8,128)(2,1)S(1)}, bf16[1,1024,192]{1,2,0:T(8,128)(2,1)}, u32[]{:S(2)}) copy-start(bf16[1,1024,192]{1,2,0:T(8,128)(2,1)} %param.26) | copy-start | bytes 1179652
  847.5 4.1 copy-start.7
  852.3 4.1 copy-start.7
  970.1 88.6 %all-to-all-start.2 = ((f32[8,1,2]{2,1,0:T(1,128)}), f32[8,1,2]{2,1,0:T(1,128)S(1)}, u32[]{:S(2)}, u32[]{:S(2)}) async-start(f32[8,1,2]{2,1,0:T(1,128)} %bitcast.14), calls=%async_computation.2 | async-start | bytes 8192 | tf_op jit(solution)/shard_map/all_to_all | solution.py:197
  1047.6 7.7 copy-start.9
  (44 other events, 116.9 us)
Sparse Core Ops, SparseCore 0:
  286.0 146.5 all-gather.4
where the time goes:
time: 1080 us; the launch traced here: 1070 us
  blocking collectives  455 us (42%)
  local copies, waits for them, and re-layouts  295 us (27%)
  other arithmetic  128 us (12%)
  starting transfers between devices  115 us (11%)
  loops' own time  40.3 us (4%)
  matrix products  19.3 us (2%)
  between operations  15.5 us (1%)
    unnamed x2, blocking collectives  223 us
    psum x1, blocking collectives, local(): b_grad, c_grad = lax.psum((b_part, c_part), ('dp', 'expert'))  124 us
    dynamic_slice x112, local copies, waits for them, and re-layouts, local(): lax.map(lambda packed: block_summary(inputs32, deltas32, cot32, packed[1]...  88 us
    all_to_all x1, starting transfers between devices, local(): lax.all_to_all(route_mine.reshape(expert_count, capacity), 'expert', spli...  77.5 us
    all_gather x3, blocking collectives, prefix(): pieces = jax.tree.map(lambda part: lax.all_gather(part, axis), value)  69.2 us
    dynamic_update_slice x96, local copies, waits for them, and re-layouts, local(): lax.map(lambda packed: block_summary(inputs32, deltas32, cot32, packed[1]...  65.6 us
    slice x1664, local copies, waits for them, and re-layouts, backward_local(): lax.associative_scan(affine_pair, (shifted, source), axis=0, reverse=True)  53.4 us
    slice x1600, local copies, waits for them, and re-layouts, forward_local(): return lax.associative_scan(affine_pair, (decays, driving), axis=0)  43.9 us

commit v1 on v0

v1 whole, which is shorter than its diff:
```python
import functools

import jax
import jax.numpy as jnp
from jax import lax
from jax.experimental import pallas as pl
from jax.experimental.pallas import tpu as pltpu
from jax.sharding import PartitionSpec as P

F32, BF16 = jnp.float32, jnp.bfloat16
MESH = pl.DeviceIdType.MESH
NDP, NSEQ, NEX = 4, 16, 8
D, HID, NST, CH, TOK = 4096, 192, 16, 256, 256
LANE = 128
WIDE = D + LANE
CA = 12 * LANE
CB = CA + 11 * LANE
CHUNKS, STEPS = 8, TOK // 8
GROUP = 4
BIG = 1e9


def get2(ref, rows):
    return jnp.concatenate([ref[0, rows, :], ref[1, rows, :]], axis=1)


def put2(ref, rows, value):
    ref[0, rows, :] = value[:, 0:LANE]
    ref[1, rows, :] = value[:, LANE:CH]


def kernel(
    cot_ref, ids_ref, wts_ref, pre_ref, w_ref, x_ref, d_ref, mc_ref, b_ref, c_ref, rate_ref,
    skip_ref, doc_ref,
    wgrad_ref, route_ref, pregrad_ref, ingrad_ref, dgrad_ref, bc_ref, rategrad_ref, skipgrad_ref,
    g, asend, arecv, asm, hid_t,
    docs, bc2d, dm2, dx2, ct2, dm, dx, ct, bx, cx, dec, car, g1, g2,
    ssum, wsum, sin2, win2, summ, gath, ret, back, sbuf, wbuf,
    bcl, bc1, bc2, bc3, rs, rsr, rgg, rp, rr1, rr2, rr3,
    ssem, rsem,
):
    y, z, e = lax.axis_index("dp"), lax.axis_index("seq"), lax.axis_index("expert")
    counter = [0]
    sent = []

    def at_seq(k):
        return lax.rem(z + k + 2 * NSEQ, NSEQ)

    def at_dp(k):
        return lax.rem(y + k + 2 * NDP, NDP)

    def at_ex(k):
        return lax.rem(e + k + 2 * NEX, NEX)

    def channel():
        counter[0] += 1
        return counter[0] - 1

    def start(src, dst, slot, device):
        copy = pltpu.make_async_remote_copy(
            src_ref=src, dst_ref=dst, send_sem=ssem.at[slot], recv_sem=rsem.at[slot],
            device_id=device, device_id_type=MESH,
        )
        copy.start()
        sent.append(copy)

    def arrive(dst, slot, device):
        pltpu.make_async_remote_copy(
            src_ref=dst, dst_ref=dst, send_sem=ssem.at[slot], recv_sem=rsem.at[slot],
            device_id=device, device_id_type=MESH,
        ).wait_recv()

    barrier = pltpu.get_barrier_semaphore()
    peers = [{"seq": at_seq(k)} for k in range(1, NSEQ)]
    peers += [{"dp": at_dp(k)} for k in range(1, NDP)]
    peers += [{"expert": at_ex(k)} for k in range(1, NEX)]
    for peer in peers:
        pl.semaphore_signal(barrier, inc=1, device_id=peer, device_id_type=MESH)

    lane8 = lax.broadcasted_iota(jnp.int32, (8, LANE), 1)
    sub8 = lax.broadcasted_iota(jnp.int32, (8, LANE), 0)
    first_id, second_id = ids_ref[:, 0:1], ids_ref[:, 1:2]
    named_first = (lane8 == first_id).astype(F32)
    named_second = (lane8 == second_id).astype(F32)
    named = jnp.maximum(named_first, named_second)
    before = jnp.zeros((8, LANE), F32)
    for t in range(7):
        before += jnp.where(sub8 > t, named[t : t + 1, :], 0.0)
    slot_of = [
        jnp.where(before == float(c), named, 0.0) for c in range(2)
    ]
    weights = wts_ref[...].astype(F32)
    pair_weight = named_first * weights[:, 0:1] + named_second * weights[:, 1:2]
    rows32 = cot_ref[...].astype(F32)
    for x in range(NEX):
        for c in range(2):
            chosen = slot_of[c][:, x : x + 1]
            asend[x, c : c + 1, 0:D] = jnp.sum(chosen * rows32, axis=0, keepdims=True)
            share = jnp.sum(
                (slot_of[c] * pair_weight)[:, x : x + 1] * jnp.ones((8, LANE), F32),
                axis=0, keepdims=True,
            )
            asend[x, c : c + 1, D:WIDE] = share

    pl.semaphore_wait(barrier, len(peers))

    a2a = [channel() for _ in range(1, NEX)]
    for k in range(1, NEX):
        start(asend.at[at_ex(k)], arecv.at[e], a2a[k - 1], {"expert": at_ex(k)})
    arecv[e] = asend[e]

    def prepare():
        doc = jnp.broadcast_to(doc_ref[...].astype(F32), (TOK, LANE))
        docs[8 : TOK + 8, :] = doc
        docs[7:8, :] = doc[0:1, :]
        keep = docs[7 : TOK + 7, :] == doc
        for h in range(2):
            cols = slice(h * LANE, (h + 1) * LANE)
            d32 = d_ref[:, cols].astype(F32)
            dm2[h] = jnp.where(keep, d32, BIG)
            dx2[h] = d32 * x_ref[:, cols].astype(F32)
            ct2[h] = mc_ref[:, cols].astype(F32)
        bc2d[0, :, 0:NST] = b_ref[...]
        bc2d[1, :, 0:NST] = c_ref[...]

    def spread():
        def body(step, _):
            rows = pl.ds(step, CHUNKS, stride=STEPS)
            dm[step] = get2(dm2, rows)
            dx[step] = get2(dx2, rows)
            ct[step] = get2(ct2, rows)
            b8, c8 = bc2d[0, rows, :], bc2d[1, rows, :]
            for n in range(NST):
                bx[step, n] = jnp.broadcast_to(b8[:, n : n + 1], (8, LANE))
                cx[step, n] = jnp.broadcast_to(c8[:, n : n + 1], (8, LANE))
            return 0

        lax.fori_loop(0, STEPS, body, 0)

    def twice(v):
        return jnp.concatenate([v, v], axis=1)

    def rate_of(n):
        return jnp.broadcast_to(rate_ref[n : n + 1, :], (8, CH)) * -1.4426950408889634

    def first_forward(group):
        names = [group * GROUP + i for i in range(GROUP)]
        scale = [rate_of(n) for n in names]

        def body(it, carry):
            carry = list(carry)
            for u in range(2):
                step = it * 2 + u
                d_now, x_now = dm[step], dx[step]
                for i, n in enumerate(names):
                    decay = jnp.exp2(d_now * scale[i])
                    dec[n, step] = decay
                    carry[i] = decay * carry[i] + twice(bx[step, n]) * x_now
            return tuple(carry)

        out = lax.fori_loop(0, STEPS // 2, body, tuple(jnp.zeros((8, CH), F32) for _ in names))
        for i, n in enumerate(names):
            put2(ssum, slice(8 * n, 8 * n + 8), out[i])

    def first_backward(group):
        names = [group * GROUP + i for i in range(GROUP)]

        def body(it, carry):
            carry = list(carry)
            for u in range(2):
                step = STEPS - 1 - (it * 2 + u)
                c_now = ct[step]
                for i, n in enumerate(names):
                    carry[i] = dec[n, step] * (twice(cx[step, n]) * c_now + carry[i])
            return tuple(carry)

        out = lax.fori_loop(0, STEPS // 2, body, tuple(jnp.zeros((8, CH), F32) for _ in names))
        for i, n in enumerate(names):
            put2(wsum, slice(8 * n, 8 * n + 8), out[i])

    through = []

    def chunk_rows(k):
        return pl.ds(k, NST, stride=CHUNKS)

    def summarize():
        total = jnp.zeros((8, CH), F32)
        total = lax.fori_loop(0, STEPS, lambda s, acc: acc + dm[s], total)
        scale = rate_ref[...] * -1.4426950408889634
        for k in range(CHUNKS):
            through.append(jnp.exp2(scale * total[k : k + 1, :]))
        state = jnp.zeros((NST, CH), F32)
        whole = jnp.ones((NST, CH), F32)
        for k in range(CHUNKS):
            state = get2(ssum, chunk_rows(k)) + through[k] * state
            whole = whole * through[k]
        adjoint = jnp.zeros((NST, CH), F32)
        for k in reversed(range(CHUNKS)):
            adjoint = get2(wsum, chunk_rows(k)) + through[k] * adjoint
        ends = jnp.concatenate([docs[8:9, :], docs[TOK + 7 : TOK + 8, :]], axis=1)
        for n in range(NST):
            summ[n, 0:1, :] = whole[n : n + 1, :]
            summ[n, 1:2, :] = state[n : n + 1, :]
            summ[n, 2:3, :] = adjoint[n : n + 1, :]
            summ[n, 3:4, :] = ends
        slots = [channel() for _ in range(1, NSEQ)]
        for k in range(1, NSEQ):
            start(summ.at[at_seq(k)], gath.at[z], slots[k - 1], {"seq": at_seq(k)})
        gath[z] = summ[z]
        return slots

    def carry_over(slots):
        for k in range(1, NSEQ):
            arrive(gath.at[at_seq(-k)], slots[k - 1], {"seq": at_seq(-k)})
        same = [jnp.zeros((1, CH), F32)]
        for p in range(1, NSEQ):
            here = gath[p, 3:4, 0:LANE]
            there = gath[p - 1, 3:4, LANE:CH]
            same.append(twice((here == there).astype(F32)))
        same.append(jnp.zeros((1, CH), F32))
        state = jnp.zeros((1, CH), F32)
        for p in range(NSEQ):
            entering = same[p] * state
            ret[p, 0:1, :] = entering
            state = gath[p, 1:2, :] + gath[p, 0:1, :] * entering
        adjoint = jnp.zeros((1, CH), F32)
        for p in reversed(range(NSEQ)):
            entering = same[p + 1] * adjoint
            ret[p, 1:2, :] = entering
            adjoint = gath[p, 2:3, :] + gath[p, 0:1, :] * entering
        slots = [channel() for _ in range(1, NSEQ)]
        for k in range(1, NSEQ):
            start(ret.at[at_seq(k)], back.at[z], slots[k - 1], {"seq": at_seq(k)})
        back[z] = ret[z]
        return slots

    def enter(slots):
        for k in range(1, NSEQ):
            arrive(back.at[at_seq(-k)], slots[k - 1], {"seq": at_seq(-k)})
        for n in range(NST):
            sbuf[n : n + 1, :] = back[n, 0:1, :]
            wbuf[n : n + 1, :] = back[n, 1:2, :]
        state = sbuf[...]
        for k in range(CHUNKS):
            put2(sin2, chunk_rows(k), state)
            state = get2(ssum, chunk_rows(k)) + through[k] * state
        adjoint = wbuf[...]
        for k in reversed(range(CHUNKS)):
            put2(win2, chunk_rows(k), adjoint)
            adjoint = get2(wsum, chunk_rows(k)) + through[k] * adjoint

    def placed(total, column, position):
        return jnp.where(lane8 == position, column, total)

    def lanes_sum(v):
        return jnp.sum(v[:, 0:LANE] + v[:, LANE:CH], axis=1, keepdims=True)

    def second_forward(group):
        names = [group * GROUP + i for i in range(GROUP)]

        def body(it, carry):
            states, sums = list(carry[:GROUP]), list(carry[GROUP:])
            for u in range(2):
                step = it * 2 + u
                x_now, c_now = dx[step], ct[step]
                for i, n in enumerate(names):
                    carried = dec[n, step] * states[i]
                    car[n, step] = carried
                    states[i] = carried + twice(bx[step, n]) * x_now
                    column = lanes_sum(states[i] * c_now)
                    sums[i // 2] = placed(sums[i // 2], column, step + (64 * (i % 2) + 32))
            return tuple(states + sums)

        init = [get2(sin2, slice(8 * n, 8 * n + 8)) for n in names]
        init += [jnp.zeros((8, LANE), F32)] * (GROUP // 2)
        out = lax.fori_loop(0, STEPS // 2, body, tuple(init))
        for i in range(GROUP // 2):
            bcl[group * (GROUP // 2) + i] = out[GROUP + i]

    def second_backward(group):
        names = [group * GROUP + i for i in range(GROUP)]
        rates = [jnp.broadcast_to(rate_ref[n : n + 1, :], (8, CH)) for n in names]

        def body(it, carry):
            adj = list(carry[:GROUP])
            grads = list(carry[GROUP : 2 * GROUP])
            sums = list(carry[2 * GROUP :])
            for u in range(2):
                step = STEPS - 1 - (it * 2 + u)
                d_now, x_now, c_now = dm[step], dx[step], ct[step]
                rows = pl.ds(pl.multiple_of(step * 8, 8), 8)
                if group == 0:
                    sum1 = sum2 = jnp.zeros((8, CH), F32)
                else:
                    sum1, sum2 = get2(g1, rows), get2(g2, rows)
                for i, n in enumerate(names):
                    here = twice(cx[step, n]) * c_now + adj[i]
                    adj[i] = dec[n, step] * here
                    product = here * car[n, step]
                    sum1 = sum1 + twice(bx[step, n]) * here
                    sum2 = sum2 + rates[i] * product
                    grads[i] = grads[i] + d_now * product
                    column = lanes_sum(here * x_now)
                    sums[i // 2] = placed(sums[i // 2], column, step + 64 * (i % 2))
                put2(g1, rows, sum1)
                put2(g2, rows, sum2)
            return tuple(adj + grads + sums)

        init = [get2(win2, slice(8 * n, 8 * n + 8)) for n in names]
        init += [jnp.zeros((8, CH), F32)] * GROUP
        init += [bcl[group * (GROUP // 2) + i] for i in range(GROUP // 2)]
        out = lax.fori_loop(0, STEPS // 2, body, tuple(init))
        for i, n in enumerate(names):
            rs[n, 0:1, :] = -jnp.sum(out[GROUP + i], axis=0, keepdims=True)
        for i in range(GROUP // 2):
            bcl[group * (GROUP // 2) + i] = out[2 * GROUP + i]

    def first_sums():
        skip = jnp.sum(mc_ref[...].astype(F32) * x_ref[...].astype(F32), axis=0, keepdims=True)
        for n in range(NST):
            rs[n, 1:2, :] = skip
        by_seq = [channel() for _ in range(1, NSEQ)]
        by_ex = [channel() for _ in range(1, NEX)]
        for k in range(1, NEX):
            start(bcl.at[at_ex(k)], bc1.at[e], by_ex[k - 1], {"expert": at_ex(k)})
        for k in range(1, NSEQ):
            start(rs.at[at_seq(k)], rsr.at[z], by_seq[k - 1], {"seq": at_seq(k)})
        bc1[e] = bcl[e]
        rsr[z] = rs[z]
        return by_seq, by_ex

    def second_sums(slots):
        by_seq, by_ex = slots
        for k in range(1, NEX):
            arrive(bc1.at[at_ex(-k)], by_ex[k - 1], {"expert": at_ex(-k)})
        tile = bc1[0]
        for k in range(1, NEX):
            tile = tile + bc1[k]
        bc2[y] = tile
        by_dp = [channel() for _ in range(1, NDP)]
        for k in range(1, NDP):
            start(bc2.at[y], bc2.at[y], by_dp[k - 1], {"dp": at_dp(k)})
        for k in range(1, NSEQ):
            arrive(rsr.at[at_seq(-k)], by_seq[k - 1], {"seq": at_seq(-k)})
        total = rsr[0]
        for p in range(1, NSEQ):
            total = total + rsr[p]
        skipgrad_ref[...] = total[1:2, :]
        rgg[z] = total[0:1, :]
        by_seq = [channel() for _ in range(1, NSEQ)]
        for k in range(1, NSEQ):
            start(rgg.at[z], rgg.at[z], by_seq[k - 1], {"seq": at_seq(k)})
        return by_seq, by_dp

    def third_sums(slots):
        by_seq, by_dp = slots
        for k in range(1, NDP):
            arrive(bc2.at[at_dp(-k)], by_dp[k - 1], {"dp": at_dp(-k)})
        bc3[e] = ((bc2[0] + bc2[1]) + bc2[2]) + bc2[3]
        by_ex = [channel() for _ in range(1, NEX)]
        for k in range(1, NEX):
            start(bc3.at[e], bc3.at[e], by_ex[k - 1], {"expert": at_ex(k)})
        return by_seq, by_ex

    def last_sums(slots):
        by_seq, by_ex = slots
        for k in range(1, NSEQ):
            arrive(rgg.at[at_seq(-k)], by_seq[k - 1], {"seq": at_seq(-k)})
        for n in range(NST):
            rategrad_ref[n : n + 1, :] = rgg[n]
        for k in range(1, NEX):
            arrive(bc3.at[at_ex(-k)], by_ex[k - 1], {"expert": at_ex(-k)})
        bc_ref[...] = bc3[...]

    def finish_scan():
        for k in range(CHUNKS):
            rows = slice(k * STEPS, (k + 1) * STEPS)
            ours = pl.ds(k, STEPS, stride=CHUNKS)
            sum1, sum2 = get2(g1, ours), get2(g2, ours)
            into = d_ref[rows, :].astype(F32) * sum1 + skip_ref[...] * mc_ref[rows, :].astype(F32)
            ingrad_ref[rows, :] = into.astype(BF16)
            dgrad_ref[rows, :] = (x_ref[rows, :].astype(F32) * sum1 - sum2).astype(BF16)

    def ring_item(name, seq, where=None):
        if name == "b":
            return g.at[y, seq, :, CA:WIDE]
        if name == "b1":
            return g.at[y, seq, :, CA:CB]
        if name == "b2":
            return g.at[y, seq, :, CB:WIDE]
        if name == "a1":
            return g.at[0:2, seq, :, 0:CA]
        return g.at[2:4, seq, :, 0:CA]

    def gather():
        plus, minus = {"seq": at_seq(1)}, {"seq": at_seq(-1)}
        up, down = {"dp": at_dp(1)}, {"dp": at_dp(-1)}
        ring = {}

        def ring_send(name, step, sign):
            seq = at_seq(-sign * (step - 1))
            ring[name, step, sign] = channel()
            start(ring_item(name, seq), ring_item(name, seq), ring[name, step, sign],
                  plus if sign > 0 else minus)

        def ring_wait(name, step, sign):
            arrive(ring_item(name, at_seq(-sign * step)), ring[name, step, sign],
                   minus if sign > 0 else plus)

        across = {}

        def across_send(dist):
            seq = at_seq(dist)
            across[dist] = [channel() for _ in range(4)]
            part = g.at[y, seq, :, CA:WIDE]
            start(part, part, across[dist][0], up)
            start(part, part, across[dist][1], down)

        def across_pass(dist):
            seq = at_seq(dist)
            slots = across[dist]
            arrive(g.at[at_dp(-1), seq, :, CA:WIDE], slots[0], down)
            half = g.at[at_dp(-1), seq, :, CA:CB]
            start(half, half, slots[2], up)
            arrive(g.at[at_dp(1), seq, :, CA:WIDE], slots[1], up)
            half = g.at[at_dp(1), seq, :, CB:WIDE]
            start(half, half, slots[3], down)

        def across_end(dist):
            seq = at_seq(dist)
            slots = across[dist]
            arrive(g.at[at_dp(2), seq, :, CA:CB], slots[2], down)
            arrive(g.at[at_dp(2), seq, :, CB:WIDE], slots[3], up)

        first = [channel() for _ in range(1, NDP)]
        mine = g.at[y, z, :, 0:CA]
        for k in range(1, NDP):
            start(mine, mine, first[k - 1], {"dp": at_dp(k)})
        ring_send("b", 1, 1)
        ring_send("b", 1, -1)
        across_send(0)
        yield
        for k in range(1, NDP):
            arrive(g.at[at_dp(-k), z, :, 0:CA], first[k - 1], {"dp": at_dp(-k)})
        for name in ("a1", "a2"):
            ring_send(name, 1, 1)
            ring_send(name, 1, -1)
        yield
        half = NSEQ // 2
        pending = [0]
        for step in range(1, half):
            for name in ("b", "a1", "a2"):
                for sign in (1, -1):
                    ring_wait(name, step, sign)
                    if step < half - 1:
                        ring_send(name, step + 1, sign)
                    elif name == "b":
                        ring_send("b1" if sign > 0 else "b2", half, sign)
                    elif (name == "a1") == (sign > 0):
                        ring_send(name, half, sign)
                if name == "b":
                    across_send(-step)
                    across_send(step)
                    for dist in pending:
                        across_pass(dist)
                    ended, pending = pending, [-step, step]
                yield
            for dist in ended:
                across_end(dist)
        ring_wait("b1", half, 1)
        ring_wait("b2", half, -1)
        across_send(half)
        yield
        for dist in pending:
            across_pass(dist)
        yield
        across_pass(half)
        ring_wait("a1", half, 1)
        ring_wait("a2", half, -1)
        for dist in pending + [half]:
            across_end(dist)

    def hidden_block(block):
        pre = pre_ref[block].reshape(256, HID).astype(F32)
        hidden = (pre * jax.nn.sigmoid(pre)).astype(BF16)
        hid_t[:, 256 * block : 256 * block + 256] = hidden.astype(F32).T.astype(BF16)

    def back_block(block, _):
        seqs = pl.ds(block * 4, 4)
        rows = g[:, seqs, :, 0:D].reshape(256, D)
        product = lax.dot_general(
            rows, w_ref[...], (((1,), (1,)), ((), ())), preferred_element_type=F32
        )
        scale = g[:, seqs, :, D:WIDE].reshape(256, LANE).astype(F32)
        scale = jnp.concatenate([scale, scale[:, 0 : HID - LANE]], axis=1)
        pre = pre_ref[:, seqs].reshape(256, HID).astype(F32)
        sig = jax.nn.sigmoid(pre)
        hidden = (pre * sig).astype(BF16).astype(F32)
        slope = sig * (1.0 + pre * (1.0 - sig))
        pregrad_ref[:, seqs] = ((scale * product) * slope).astype(BF16).reshape(4, 4, 16, HID)
        column = jnp.sum(hidden * product, axis=1, keepdims=True)
        eye = lax.broadcasted_iota(jnp.int32, (LANE, LANE), 0) == lax.broadcasted_iota(
            jnp.int32, (LANE, LANE), 1
        )
        for h in range(2):
            part = column[h * LANE : (h + 1) * LANE, :]
            rp[block, h : h + 1, :] = jnp.sum(jnp.where(eye, part, 0.0), axis=0, keepdims=True)
        return 0

    def weight_tile(tile, _):
        width = 512
        cols = pl.ds(pl.multiple_of(tile * width, width), width)
        scale = g[:, :, :, D:WIDE].reshape(1024, LANE).astype(F32)
        scale = jnp.concatenate([scale] * (width // LANE), axis=1)
        rows = g[:, :, :, cols].reshape(1024, width).astype(F32)
        scaled = (rows * scale).astype(BF16)
        wgrad_ref[:, cols] = jnp.dot(
            hid_t[...], scaled, preferred_element_type=F32
        ).astype(BF16)
        return 0

    prepare()
    for k in range(1, NEX):
        arrive(arecv.at[at_ex(-k)], a2a[k - 1], {"expert": at_ex(-k)})
    for q in range(NEX):
        asm[2 * q : 2 * q + 2, :] = arecv[q]
    g[y, z] = asm[...].astype(BF16)

    gathering = gather()
    tick = functools.partial(next, gathering, None)
    tick()
    spread()
    tick()
    for group in range(NST // GROUP):
        first_forward(group)
        first_backward(group)
        tick()
    slots = summarize()
    tick()
    hidden_block(0)
    hidden_block(1)
    tick()
    slots = carry_over(slots)
    tick()
    hidden_block(2)
    hidden_block(3)
    tick()
    enter(slots)
    for group in range(NST // GROUP):
        tick()
        second_forward(group)
    for group in range(NST // GROUP):
        tick()
        second_backward(group)
    tick()
    slots = first_sums()
    finish_scan()
    tick()
    slots = second_sums(slots)
    tick()
    slots = third_sums(slots)
    tick()
    last_sums(slots)
    for _ in gathering:
        pass

    lax.fori_loop(0, 4, back_block, 0)
    by_seq = [channel() for _ in range(1, NSEQ)]
    for k in range(1, NSEQ):
        start(rp.at[at_seq(k) // 4], rr1.at[z], by_seq[k - 1], {"seq": at_seq(k)})
    rr1[z] = rp[z // 4]
    lax.fori_loop(0, 4, weight_tile, 0)
    for k in range(1, NSEQ):
        arrive(rr1.at[at_seq(-k)], by_seq[k - 1], {"seq": at_seq(-k)})
    total = rr1[0]
    for p in range(1, NSEQ):
        total = total + rr1[p]
    rr2[y] = total
    by_dp = [channel() for _ in range(1, NDP)]
    for k in range(1, NDP):
        start(rr2.at[y], rr2.at[y], by_dp[k - 1], {"dp": at_dp(k)})
    lax.fori_loop(4, 6, weight_tile, 0)
    for k in range(1, NDP):
        arrive(rr2.at[at_dp(-k)], by_dp[k - 1], {"dp": at_dp(-k)})
    rr3[e] = ((rr2[0] + rr2[1]) + rr2[2]) + rr2[3]
    by_ex = [channel() for _ in range(1, NEX)]
    for k in range(1, NEX):
        start(rr3.at[e], rr3.at[e], by_ex[k - 1], {"expert": at_ex(k)})
    lax.fori_loop(6, 8, weight_tile, 0)
    for k in range(1, NEX):
        arrive(rr3.at[at_ex(-k)], by_ex[k - 1], {"expert": at_ex(-k)})

    row_of = lax.broadcasted_iota(jnp.int32, (2, LANE), 0)
    lane_of = lax.broadcasted_iota(jnp.int32, (2, LANE), 1)
    base = (y % 2) * 64 + (z % 4) * 16 + e * 2
    picked = jnp.zeros((8, LANE), F32)
    for c in range(2):
        values = jnp.zeros((1, LANE), F32)
        for x in range(NEX):
            here = (row_of == y // 2) & (lane_of == base + c)
            value = jnp.sum(
                jnp.sum(jnp.where(here, rr3[x], 0.0), axis=0, keepdims=True),
                axis=1, keepdims=True,
            )
            values = jnp.where(lane8[0:1, :] == x, value, values)
        picked = picked + slot_of[c] * values
    route_first = jnp.sum(picked * named_first, axis=1, keepdims=True)
    route_second = jnp.sum(picked * named_second, axis=1, keepdims=True)
    route_ref[...] = jnp.where(lane8 == 0, route_first, route_second)[:, 0:2]

    for copy in sent:
        copy.wait_send()


def local(
    moe_cotangent, route_ids, route_weights, saved_pre, w_down, inputs, deltas, mamba_cotangent,
    b_proj, c_proj, decay_rates, skip_gain, documents,
):
    vmem = pl.BlockSpec(memory_space=pltpu.VMEM)

    def out(shape, dtype):
        return jax.ShapeDtypeStruct(shape, dtype)

    def f32(*shape):
        return pltpu.VMEM(shape, F32)

    copies = 320
    wgrad, route, pregrad, ingrad, dgrad, bc, rategrad, skipgrad = pl.pallas_call(
        kernel,
        out_shape=(
            out((HID, D), BF16),
            out((8, 2), F32),
            out((NDP, NSEQ, 16, HID), BF16),
            out((TOK, CH), BF16),
            out((TOK, CH), BF16),
            out((8, 8, LANE), F32),
            out((NST, CH), F32),
            out((1, CH), F32),
        ),
        in_specs=[vmem] * 13,
        out_specs=[vmem] * 8,
        scratch_shapes=[
            pltpu.VMEM((NDP, NSEQ, 16, WIDE), BF16),
            f32(NEX, 2, WIDE), f32(NEX, 2, WIDE), f32(16, WIDE),
            pltpu.VMEM((HID, 1024), BF16),
            f32(TOK + 8, LANE),
            f32(2, TOK, LANE), f32(2, TOK, LANE), f32(2, TOK, LANE), f32(2, TOK, LANE),
            f32(STEPS, 8, CH), f32(STEPS, 8, CH), f32(STEPS, 8, CH),
            f32(STEPS, NST, 8, LANE), f32(STEPS, NST, 8, LANE),
            f32(NST, STEPS, 8, CH), f32(NST, STEPS, 8, CH),
            f32(2, TOK, LANE), f32(2, TOK, LANE),
            f32(2, TOK // 2, LANE), f32(2, TOK // 2, LANE),
            f32(2, TOK // 2, LANE), f32(2, TOK // 2, LANE),
            f32(NST, 4, CH), f32(NSEQ, 4, CH), f32(NSEQ, 2, CH), f32(NST, 2, CH),
            f32(NST, CH), f32(NST, CH),
            f32(8, 8, LANE), f32(8, 8, LANE), f32(NDP, 8, LANE), f32(8, 8, LANE),
            f32(NST, 2, CH), f32(NSEQ, 2, CH), f32(NST, 1, CH),
            f32(4, 2, LANE), f32(NSEQ, 2, LANE), f32(NDP, 2, LANE), f32(NEX, 2, LANE),
            pltpu.SemaphoreType.DMA((copies,)),
            pltpu.SemaphoreType.DMA((copies,)),
        ],
        compiler_params=pltpu.CompilerParams(
            collective_id=0, has_side_effects=True, vmem_limit_bytes=56 * 1024 * 1024
        ),
    )(
        moe_cotangent, route_ids, route_weights,
        saved_pre.reshape(NDP, NSEQ, 16, HID), w_down.reshape(HID, D),
        inputs, deltas, mamba_cotangent, b_proj, c_proj, decay_rates,
        skip_gain.reshape(1, CH), documents.reshape(TOK, 1),
    )
    both = bc.reshape(8, CHUNKS, 2, 2, STEPS).transpose(3, 1, 4, 0, 2).reshape(2, TOK, NST)
    return (
        wgrad.reshape(1, HID, D),
        route,
        pregrad.reshape(1, 1024, HID),
        ingrad,
        dgrad,
        both[0],
        both[1],
        rategrad,
        skipgrad.reshape(CH),
    )


def solution(mesh):
    return jax.shard_map(
        local,
        mesh=mesh,
        in_specs=(
            P(("dp", "seq", "expert"), None),
            P(("dp", "seq", "expert"), None),
            P(("dp", "seq", "expert"), None),
            P("expert", None, ("dp", "seq")),
            P("expert", ("dp", "seq"), None),
            P("seq", ("dp", "expert")),
            P("seq", ("dp", "expert")),
            P("seq", ("dp", "expert")),
            P("seq", None),
            P("seq", None),
            P(None, ("dp", "expert")),
            P(("dp", "expert")),
            P("seq"),
        ),
        out_specs=(
            P("expert", ("dp", "seq"), None),
            P(("dp", "seq", "expert"), None),
            P("expert", None, ("dp", "seq")),
            P("seq", ("dp", "expert")),
            P("seq", ("dp", "expert")),
            P("seq", None),
            P("seq", None),
            P(None, ("dp", "expert")),
            P(("dp", "expert")),
        ),
        check_vma=False,
    )
```

time: 1080 us -> 146 us (0.14); the launches traced: 1070 us -> 146 us
  blocking collectives: 455 us -> 0 us
  local copies, waits for them, and re-layouts: 295 us -> 18.5 us
  other arithmetic: 128 us -> 0 us
  Pallas kernels: 0 us -> 126 us
  starting transfers between devices: 115 us -> 0 us
  loops' own time: 40.3 us -> 0 us
  matrix products: 19.3 us -> 0 us
  between operations: 15.5 us -> 0.7 us
    unnamed x2 -> x0, blocking collectives: 223 us -> none
    psum x2 -> x0, blocking collectives: 163 us -> none  [the longest x1 124 us: local(): b_grad, c_grad = lax.psum((b_part, c_part), ('dp', 'expert'))]
    pallas_call x0 -> x1, Pallas kernels: none -> 126 us  [local(): pl.pallas_call(kernel, out_shape=(out((HID, D), BF16), out((8, 2), F32),...]
    all_to_all x3 -> x0, starting transfers between devices: 114 us -> none  [the longest x1 77.5 us: local(): lax.all_to_all(route_mine.reshape(expert_count, capacity), 'expert', spli...]
    slice x3329 -> x3, local copies, waits for them, and re-layouts: 99.3 us -> 0.11 us  [the longest x2 0.11 us: local(): both[1]]
    dynamic_slice x112 -> x0, local copies, waits for them, and re-layouts: 88 us -> none  [local(): lax.map(lambda packed: block_summary(inputs32, deltas32, cot32, packed[1]...]
    all_gather x3 -> x0, blocking collectives: 69.2 us -> none  [prefix(): pieces = jax.tree.map(lambda part: lax.all_gather(part, axis), value)]
    dynamic_update_slice x98 -> x0, local copies, waits for them, and re-layouts: 65.7 us -> none  [the longest x96 65.6 us: local(): lax.map(lambda packed: block_summary(inputs32, deltas32, cot32, packed[1]...]
where the time goes in v1:
time: 146 us
  Pallas kernels  126 us (86%)
  local copies, waits for them, and re-layouts  18.5 us (13%)
    pallas_call x1, Pallas kernels, local(): pl.pallas_call(kernel, out_shape=(out((HID, D), BF16), out((8, 2), F32),...  126 us
    unnamed x22, local copies, waits for them, and re-layouts  14.6 us

profile of v1, /device:TPU:1, one launch (start us, length us, event | category | flops | bytes accessed | tf_op | source)
XLA Modules:
  0.0 145.7 jit_solution(6045030461965088579)
XLA Ops:
  0.6 1.3 copy.33.wts_ref
  2.0 1.3 copy.32.ids_ref
  3.3 1.5 %copy.34.b_ref = f32[256,16]{1,0:T(8,128)} copy(f32[256,16]{0,1:T(8,128)} %param.21) | data formatting | bytes 32768 | tf_op args[8]
  4.8 1.5 %copy.35.c_ref = f32[256,16]{1,0:T(8,128)} copy(f32[256,16]{0,1:T(8,128)} %param.22) | data formatting | bytes 32768 | tf_op args[9]
  6.2 1.5 %copy.36.doc_ref = s32[256,1]{1,0:T(8,128)} copy(s32[256,1]{0,1:T(1,128)} %bitcast.21) | data formatting | bytes 2048 | tf_op jit(solution)/shard_map/reshape | solution.py:669
  7.7 2.0 %copy.31 = bf16[1,1024,192]{2,1,0:T(8,128)(2,1)} copy(bf16[1,1024,192]{1,2,0:T(8,128)(2,1)} %param.16) | data formatting | bytes 786432 | tf_op args[3]
  9.7 126.4 %shard_map.196 = (bf16[192,4096]{1,0:T(8,128)(2,1)}, f32[8,2]{1,0:T(8,128)}, bf16[4,16,16,192]{3,2,1,0:T(8,128)(2,1)}, bf16[256,256]{1,0:T(8,128)(2,1)}, bf16[25...) custom-call(bf16[8,4096]{1,0:T(8,128)(2,1)} %cot_ref.1, ...), custom_call_target="tpu_custom_call" | custom-call | tf_op jit(solution)/shard_map/pallas_call | solution.py:628
  136.2 0.0 copy-start
  136.2 1.4 copy.39
  137.6 0.9 reshape.53
  138.5 0.1 fusion
  138.6 0.7 squeeze.7
  139.3 0.7 squeeze.6
  140.0 2.0 %copy.40 = bf16[1,1024,192]{1,2,0:T(8,128)(2,1)} copy(bf16[1,1024,192]{2,1,0:T(8,128)(2,1)} %bitcast.19) | data formatting | bytes 786432
  142.0 0.0 copy-done
  142.0 0.0 copy-start.2
  142.0 0.0 copy-start.1
  142.0 0.0 copy-start.3
  142.0 0.0 copy-start.4
  142.0 1.1 copy.46
  143.2 0.0 copy-done.2
  143.2 0.7 copy.47
  143.8 0.0 copy-done.1
  143.8 0.7 copy.48
  144.5 0.0 copy-done.3
  144.5 0.6 copy.49
  145.1 0.0 copy-done.4
  145.1 0.6 copy.50
  (2 shorter events, 0.0 us)
Async XLA Ops:
  136.2 5.8 %copy-start = (bf16[192,4096]{1,0:T(8,128)(2,1)S(1)}, bf16[192,4096]{1,0:T(8,128)(2,1)}, u32[]{:S(2)}) copy-start(bf16[192,4096]{1,0:T(8,128)(2,1)} %get-tuple-element.17) | copy-start | bytes 4718596
  142.0 1.2 copy-start.2
  142.0 1.8 %copy-start.1 = (bf16[256,256]{1,0:T(8,128)(2,1)S(1)}, bf16[256,256]{1,0:T(8,128)(2,1)}, u32[]{:S(2)}) copy-start(bf16[256,256]{1,0:T(8,128)(2,1)} %get-tuple-element.58) | copy-start | bytes 393220
  142.0 2.5 %copy-start.3 = (f32[16,256]{1,0:T(8,128)S(1)}, f32[16,256]{1,0:T(8,128)}, u32[]{:S(2)}) copy-start(f32[16,256]{1,0:T(8,128)} %get-tuple-element.61) | copy-start | bytes 49156
  142.0 3.1 %copy-start.4 = (f32[1,256]{1,0:T(1,128)S(1)}, f32[1,256]{1,0:T(1,128)}, u32[]{:S(2)}) copy-start(f32[1,256]{1,0:T(1,128)} %get-tuple-element.24) | copy-start | bytes 3076

commit v2 on v1

--- a/solution.py
+++ b/solution.py
@@ -30,15 +30,33 @@
 
 
 def kernel(
-    cot_ref, ids_ref, wts_ref, pre_ref, w_ref, x_ref, d_ref, mc_ref, b_ref, c_ref, rate_ref,
-    skip_ref, doc_ref,
-    wgrad_ref, route_ref, pregrad_ref, ingrad_ref, dgrad_ref, bc_ref, rategrad_ref, skipgrad_ref,
-    g, asend, arecv, asm, hid_t,
-    docs, bc2d, dm2, dx2, ct2, dm, dx, ct, bx, cx, dec, car, g1, g2,
-    ssum, wsum, sin2, win2, summ, gath, ret, back, sbuf, wbuf,
-    bcl, bc1, bc2, bc3, rs, rsr, rgg, rp, rr1, rr2, rr3,
-    ssem, rsem,
+    cot_ref, ids_ref, wts_ref, *refs
 ):
+    count_in, count_out = 10, 9
+    far_in, refs = refs[:count_in], refs[count_in:]
+    far_out, refs = refs[:count_out], refs[count_out:]
+    near_in, refs = refs[:count_in], refs[count_in:]
+    near_out, refs = refs[:count_out], refs[count_out:]
+    pre_ref, w_ref, x_ref, d_ref, mc_ref, b_ref, c_ref, rate_ref, skip_ref, doc_ref = near_in
+    (
+        wgrad_ref, route_ref, pregrad_ref, ingrad_ref, dgrad_ref, bgrad_ref, cgrad_ref,
+        rategrad_ref, skipgrad_ref,
+    ) = near_out
+    (
+        g, asend, arecv, asm, hid_t, hid_r, slope_t, backs,
+        docs, bc2d, dm2, dx2, ct2, dm, dx, ct, bx, cx, dec, car, g1, g2,
+        ssum, wsum, sin2, win2, summ, gath, ret, back, sbuf, wbuf,
+        bcl, bc1, bc2, bc3, rs, rsr, rgg, rp, rr1, rr2, rr3,
+        ssem, rsem, isem, osem, tsem,
+    ) = refs
+    loads = [
+        pltpu.make_async_copy(far, near, isem.at[i])
+        for i, (far, near) in enumerate(zip(far_in, near_in))
+    ]
+    stores = [None] + [
+        pltpu.make_async_copy(near_out[i], far_out[i], osem.at[i]) for i in range(1, count_out)
+    ]
+
     y, z, e = lax.axis_index("dp"), lax.axis_index("seq"), lax.axis_index("expert")
     counter = [0]
     sent = []
@@ -77,11 +95,21 @@
     for peer in peers:
         pl.semaphore_signal(barrier, inc=1, device_id=peer, device_id_type=MESH)
 
+    for i in (2, 3, 4, 5, 6, 7, 8, 9, 0, 1):
+        loads[i].start()
+
     lane8 = lax.broadcasted_iota(jnp.int32, (8, LANE), 1)
     sub8 = lax.broadcasted_iota(jnp.int32, (8, LANE), 0)
-    first_id, second_id = ids_ref[:, 0:1], ids_ref[:, 1:2]
-    named_first = (lane8 == first_id).astype(F32)
-    named_second = (lane8 == second_id).astype(F32)
+    eye8 = lane8[:, 0:8] == sub8[:, 0:8]
+
+    def column(row):
+        return jnp.sum(
+            jnp.where(eye8, jnp.broadcast_to(row, (8, 8)), 0.0), axis=1, keepdims=True
+        )
+
+    lanes32 = lane8.astype(F32)
+    named_first = (lanes32 == column(ids_ref[0:1, :].astype(F32))).astype(F32)
+    named_second = (lanes32 == column(ids_ref[1:2, :].astype(F32))).astype(F32)
     named = jnp.maximum(named_first, named_second)
     before = jnp.zeros((8, LANE), F32)
     for t in range(7):
@@ -90,7 +118,7 @@
         jnp.where(before == float(c), named, 0.0) for c in range(2)
     ]
     weights = wts_ref[...].astype(F32)
-    pair_weight = named_first * weights[:, 0:1] + named_second * weights[:, 1:2]
+    pair_weight = named_first * column(weights[0:1, :]) + named_second * column(weights[1:2, :])
     rows32 = cot_ref[...].astype(F32)
     for x in range(NEX):
         for c in range(2):
@@ -110,8 +138,10 @@
     arecv[e] = asend[e]
 
     def prepare():
-        doc = jnp.broadcast_to(doc_ref[...].astype(F32), (TOK, LANE))
-        docs[8 : TOK + 8, :] = doc
+        for h in range(2):
+            row = doc_ref[:, h * LANE : (h + 1) * LANE].astype(F32)
+            docs[8 + h * LANE : 8 + (h + 1) * LANE, :] = jnp.broadcast_to(row, (LANE, LANE)).T
+        doc = docs[8 : TOK + 8, :]
         docs[7:8, :] = doc[0:1, :]
         keep = docs[7 : TOK + 7, :] == doc
         for h in range(2):
@@ -120,8 +150,9 @@
             dm2[h] = jnp.where(keep, d32, BIG)
             dx2[h] = d32 * x_ref[:, cols].astype(F32)
             ct2[h] = mc_ref[:, cols].astype(F32)
-        bc2d[0, :, 0:NST] = b_ref[...]
-        bc2d[1, :, 0:NST] = c_ref[...]
+            for i, ref in enumerate((b_ref, c_ref)):
+                tall = [ref[:, cols], jnp.zeros((LANE - NST, LANE), F32)]
+                bc2d[i, cols, :] = jnp.concatenate(tall, axis=0).T
 
     def spread():
         def body(step, _):
@@ -249,8 +280,12 @@
             put2(win2, chunk_rows(k), adjoint)
             adjoint = get2(wsum, chunk_rows(k)) + through[k] * adjoint
 
-    def placed(total, column, position):
-        return jnp.where(lane8 == position, column, total)
+    place = (sub8 % 4) * STEPS
+
+    def in_rows(n, first, value):
+        at = first + 2 * (n % 2)
+        bcl[n // 2, at : at + 1, :] = jnp.sum(value[0:4, :], axis=0, keepdims=True)
+        bcl[n // 2, at + 1 : at + 2, :] = jnp.sum(value[4:8, :], axis=0, keepdims=True)
 
     def lanes_sum(v):
         return jnp.sum(v[:, 0:LANE] + v[:, LANE:CH], axis=1, keepdims=True)
@@ -263,19 +298,20 @@
             for u in range(2):
                 step = it * 2 + u
                 x_now, c_now = dx[step], ct[step]
+                here = lane8 == place + step
                 for i, n in enumerate(names):
                     carried = dec[n, step] * states[i]
                     car[n, step] = carried
                     states[i] = carried + twice(bx[step, n]) * x_now
-                    column = lanes_sum(states[i] * c_now)
-                    sums[i // 2] = placed(sums[i // 2], column, step + (64 * (i % 2) + 32))
+                    total = lanes_sum(states[i] * c_now)
+                    sums[i] = jnp.where(here, total, sums[i])
             return tuple(states + sums)
 
         init = [get2(sin2, slice(8 * n, 8 * n + 8)) for n in names]
-        init += [jnp.zeros((8, LANE), F32)] * (GROUP // 2)
+        init += [jnp.zeros((8, LANE), F32)] * GROUP
         out = lax.fori_loop(0, STEPS // 2, body, tuple(init))
-        for i in range(GROUP // 2):
-            bcl[group * (GROUP // 2) + i] = out[GROUP + i]
+        for i, n in enumerate(names):
+            in_rows(n, 4, out[GROUP + i])
 
     def second_backward(group):
         names = [group * GROUP + i for i in range(GROUP)]
@@ -289,6 +325,7 @@
                 step = STEPS - 1 - (it * 2 + u)
                 d_now, x_now, c_now = dm[step], dx[step], ct[step]
                 rows = pl.ds(pl.multiple_of(step * 8, 8), 8)
+                spot = lane8 == place + step
                 if group == 0:
                     sum1 = sum2 = jnp.zeros((8, CH), F32)
                 else:
@@ -300,20 +337,18 @@
                     sum1 = sum1 + twice(bx[step, n]) * here
                     sum2 = sum2 + rates[i] * product
                     grads[i] = grads[i] + d_now * product
-                    column = lanes_sum(here * x_now)
-                    sums[i // 2] = placed(sums[i // 2], column, step + 64 * (i % 2))
+                    sums[i] = jnp.where(spot, lanes_sum(here * x_now), sums[i])
                 put2(g1, rows, sum1)
                 put2(g2, rows, sum2)
             return tuple(adj + grads + sums)
 
         init = [get2(win2, slice(8 * n, 8 * n + 8)) for n in names]
         init += [jnp.zeros((8, CH), F32)] * GROUP
-        init += [bcl[group * (GROUP // 2) + i] for i in range(GROUP // 2)]
+        init += [jnp.zeros((8, LANE), F32)] * GROUP
         out = lax.fori_loop(0, STEPS // 2, body, tuple(init))
         for i, n in enumerate(names):
             rs[n, 0:1, :] = -jnp.sum(out[GROUP + i], axis=0, keepdims=True)
-        for i in range(GROUP // 2):
-            bcl[group * (GROUP // 2) + i] = out[2 * GROUP + i]
+            in_rows(n, 0, out[2 * GROUP + i])
 
     def first_sums():
         skip = jnp.sum(mc_ref[...].astype(F32) * x_ref[...].astype(F32), axis=0, keepdims=True)
@@ -370,7 +405,11 @@
             rategrad_ref[n : n + 1, :] = rgg[n]
         for k in range(1, NEX):
             arrive(bc3.at[at_ex(-k)], by_ex[k - 1], {"expert": at_ex(-k)})
-        bc_ref[...] = bc3[...]
+        for n in range(NST):
+            for h in range(2):
+                at, cols = 2 * (n % 2) + h, slice(h * LANE, (h + 1) * LANE)
+                bgrad_ref[n : n + 1, cols] = bc3[n // 2, at : at + 1, :]
+                cgrad_ref[n : n + 1, cols] = bc3[n // 2, at + 4 : at + 5, :]
 
     def finish_scan():
         for k in range(CHUNKS):
@@ -447,7 +486,7 @@
             ring_send(name, 1, -1)
         yield
         half = NSEQ // 2
-        pending = [0]
+        pending, passed = [0], []
         for step in range(1, half):
             for name in ("b", "a1", "a2"):
                 for sign in (1, -1):
@@ -461,51 +500,76 @@
                 if name == "b":
                     across_send(-step)
                     across_send(step)
+                elif name == "a1":
                     for dist in pending:
                         across_pass(dist)
-                    ended, pending = pending, [-step, step]
+                else:
+                    for dist in passed:
+                        across_end(dist)
+                    seq_block(passed)
+                    pending, passed = [-step, step], pending
                 yield
-            for dist in ended:
-                across_end(dist)
         ring_wait("b1", half, 1)
         ring_wait("b2", half, -1)
         across_send(half)
         yield
         for dist in pending:
             across_pass(dist)
+        for dist in passed:
+            across_end(dist)
+        seq_block(passed)
         yield
         across_pass(half)
         ring_wait("a1", half, 1)
         ring_wait("a2", half, -1)
-        for dist in pending + [half]:
+        for dist in pending:
             across_end(dist)
+        seq_block(pending)
+        across_end(half)
+        seq_block([half])
 
     def hidden_block(block):
-        pre = pre_ref[block].reshape(256, HID).astype(F32)
-        hidden = (pre * jax.nn.sigmoid(pre)).astype(BF16)
-        hid_t[:, 256 * block : 256 * block + 256] = hidden.astype(F32).T.astype(BF16)
-
-    def back_block(block, _):
-        seqs = pl.ds(block * 4, 4)
-        rows = g[:, seqs, :, 0:D].reshape(256, D)
+        cols = slice(block * 256, (block + 1) * 256)
+        pre = pre_ref[:, cols].astype(F32)
+        sig = jax.nn.sigmoid(pre)
+        hidden = (pre * sig).astype(BF16)
+        hid_t[:, cols] = hidden
+        slope_t[:, cols] = sig * (1.0 + pre * (1.0 - sig))
+        tall = jnp.concatenate([hidden.astype(F32), jnp.zeros((256 - HID, 256), F32)], axis=0)
+        hid_r[block] = tall.T[:, 0:HID].reshape(NSEQ, 16, HID)
+
+    route_slots = [None] + [channel() for _ in range(1, NSEQ)]
+    row64 = lax.broadcasted_iota(jnp.int32, (64, LANE), 0)
+    eye64 = lax.broadcasted_iota(jnp.int32, (64, LANE), 1) == row64
+
+    def seq_block(dists):
+        if not dists:
+            return
+        seqs = [at_seq(dist) for dist in dists]
+        rows = [g[:, seq, :, 0:D].reshape(64, D) for seq in seqs]
+        rows = rows[0] if len(rows) == 1 else jnp.concatenate(rows, axis=0)
         product = lax.dot_general(
             rows, w_ref[...], (((1,), (1,)), ((), ())), preferred_element_type=F32
         )
-        scale = g[:, seqs, :, D:WIDE].reshape(256, LANE).astype(F32)
-        scale = jnp.concatenate([scale, scale[:, 0 : HID - LANE]], axis=1)
-        pre = pre_ref[:, seqs].reshape(256, HID).astype(F32)
-        sig = jax.nn.sigmoid(pre)
-        hidden = (pre * sig).astype(BF16).astype(F32)
-        slope = sig * (1.0 + pre * (1.0 - sig))
-        pregrad_ref[:, seqs] = ((scale * product) * slope).astype(BF16).reshape(4, 4, 16, HID)
-        column = jnp.sum(hidden * product, axis=1, keepdims=True)
-        eye = lax.broadcasted_iota(jnp.int32, (LANE, LANE), 0) == lax.broadcasted_iota(
-            jnp.int32, (LANE, LANE), 1
-        )
-        for h in range(2):
-            part = column[h * LANE : (h + 1) * LANE, :]
-            rp[block, h : h + 1, :] = jnp.sum(jnp.where(eye, part, 0.0), axis=0, keepdims=True)
-        return 0
+        for i, (dist, seq) in enumerate(zip(dists, seqs)):
+            mine = product[64 * i : 64 * i + 64, :]
+            scale = g[:, seq, :, D:WIDE].reshape(64, LANE).astype(F32)
+            scale = jnp.concatenate([scale, scale[:, 0 : HID - LANE]], axis=1)
+            backs[:, seq] = (scale * mine).reshape(NDP, 16, HID)
+            total = jnp.sum(hid_r[:, seq].reshape(64, HID) * mine, axis=1, keepdims=True)
+            line = jnp.sum(jnp.where(eye64, total, 0.0), axis=0, keepdims=True)
+            if dist == 0:
+                rr1[z] = line
+            else:
+                rp[seq] = line
+                start(rp.at[seq], rr1.at[z], route_slots[dist % NSEQ], {"seq": seq})
+
+    def slopes():
+        for block in range(NDP):
+            cols = slice(block * 256, (block + 1) * 256)
+            tall = backs[block].reshape(256, HID)
+            wide = jnp.concatenate([tall, jnp.zeros((256, 256 - HID), F32)], axis=1).T
+            pregrad_ref[:, cols] = (wide[0:HID, :] * slope_t[:, cols]).astype(BF16)
 
     def weight_tile(tile, _):
         width = 512
@@ -517,9 +581,22 @@
         wgrad_ref[:, cols] = jnp.dot(
             hid_t[...], scaled, preferred_element_type=F32
         ).astype(BF16)
+        pltpu.make_async_copy(
+            wgrad_ref.at[:, cols], far_out[0].at[:, cols], tsem.at[tile]
+        ).start()
         return 0
 
+    def weight_done(tile, _):
+        cols = pl.ds(pl.multiple_of(tile * 512, 512), 512)
+        pltpu.make_async_copy(
+            wgrad_ref.at[:, cols], far_out[0].at[:, cols], tsem.at[tile]
+        ).wait()
+        return 0
+
+    for i in range(2, 10):
+        loads[i].wait()
     prepare()
+    spread()
     for k in range(1, NEX):
         arrive(arecv.at[at_ex(-k)], a2a[k - 1], {"expert": at_ex(-k)})
     for q in range(NEX):
@@ -529,21 +606,19 @@
     gathering = gather()
     tick = functools.partial(next, gathering, None)
     tick()
-    spread()
-    tick()
     for group in range(NST // GROUP):
         first_forward(group)
         first_backward(group)
+    slots = summarize()
+    tick()
+    for i in range(2):
+        loads[i].wait()
+    for block in range(NDP):
+        hidden_block(block)
         tick()
-    slots = summarize()
-    tick()
-    hidden_block(0)
-    hidden_block(1)
-    tick()
     slots = carry_over(slots)
     tick()
-    hidden_block(2)
-    hidden_block(3)
+    tick()
     tick()
     enter(slots)
     for group in range(NST // GROUP):
@@ -555,23 +630,26 @@
     tick()
     slots = first_sums()
     finish_scan()
+    stores[3].start()
+    stores[4].start()
+    tick()
+    tick()
     tick()
     slots = second_sums(slots)
+    stores[8].start()
+    tick()
+    tick()
     tick()
     slots = third_sums(slots)
-    tick()
-    last_sums(slots)
     for _ in gathering:
         pass
 
-    lax.fori_loop(0, 4, back_block, 0)
-    by_seq = [channel() for _ in range(1, NSEQ)]
+    lax.fori_loop(0, 4, weight_tile, 0)
+    last_sums(slots)
+    for i in (5, 6, 7):
+        stores[i].start()
     for k in range(1, NSEQ):
-        start(rp.at[at_seq(k) // 4], rr1.at[z], by_seq[k - 1], {"seq": at_seq(k)})
-    rr1[z] = rp[z // 4]
-    lax.fori_loop(0, 4, weight_tile, 0)
-    for k in range(1, NSEQ):
-        arrive(rr1.at[at_seq(-k)], by_seq[k - 1], {"seq": at_seq(-k)})
+        arrive(rr1.at[at_seq(-k)], route_slots[k], {"seq": at_seq(-k)})
     total = rr1[0]
     for p in range(1, NSEQ):
         total = total + rr1[p]
@@ -579,37 +657,69 @@
     by_dp = [channel() for _ in range(1, NDP)]
     for k in range(1, NDP):
         start(rr2.at[y], rr2.at[y], by_dp[k - 1], {"dp": at_dp(k)})
-    lax.fori_loop(4, 6, weight_tile, 0)
+    slopes()
+    stores[2].start()
     for k in range(1, NDP):
         arrive(rr2.at[at_dp(-k)], by_dp[k - 1], {"dp": at_dp(-k)})
     rr3[e] = ((rr2[0] + rr2[1]) + rr2[2]) + rr2[3]
     by_ex = [channel() for _ in range(1, NEX)]
     for k in range(1, NEX):
         start(rr3.at[e], rr3.at[e], by_ex[k - 1], {"expert": at_ex(k)})
-    lax.fori_loop(6, 8, weight_tile, 0)
+    lax.fori_loop(4, 8, weight_tile, 0)
     for k in range(1, NEX):
         arrive(rr3.at[at_ex(-k)], by_ex[k - 1], {"expert": at_ex(-k)})
 
-    row_of = lax.broadcasted_iota(jnp.int32, (2, LANE), 0)
-    lane_of = lax.broadcasted_iota(jnp.int32, (2, LANE), 1)
-    base = (y % 2) * 64 + (z % 4) * 16 + e * 2
+    base = y * 16 + e * 2
     picked = jnp.zeros((8, LANE), F32)
     for c in range(2):
         values = jnp.zeros((1, LANE), F32)
         for x in range(NEX):
-            here = (row_of == y // 2) & (lane_of == base + c)
-            value = jnp.sum(
-                jnp.sum(jnp.where(here, rr3[x], 0.0), axis=0, keepdims=True),
-                axis=1, keepdims=True,
-            )
+            here = lane8[0:1, :] == base + c
+            value = jnp.sum(jnp.where(here, rr3[x], 0.0), axis=1, keepdims=True)
             values = jnp.where(lane8[0:1, :] == x, value, values)
         picked = picked + slot_of[c] * values
-    route_first = jnp.sum(picked * named_first, axis=1, keepdims=True)
-    route_second = jnp.sum(picked * named_second, axis=1, keepdims=True)
-    route_ref[...] = jnp.where(lane8 == 0, route_first, route_second)[:, 0:2]
-
+    for k, names in enumerate((named_first, named_second)):
+        total = jnp.sum(picked * names, axis=1, keepdims=True)
+        line = jnp.sum(jnp.where(lane8 == sub8, total, 0.0), axis=0, keepdims=True)
+        route_ref[k : k + 1, :] = line[:, 0:8]
+
+    stores[1].start()
+    lax.fori_loop(0, 8, weight_done, 0)
+    for copy in stores[1:]:
+        copy.wait()
     for copy in sent:
         copy.wait_send()
+
+
+def hand_over(*arrays):
+    count = len(arrays)
+
+    def body(*refs):
+        sources, targets, held = refs[:count], refs[count : 2 * count], refs[2 * count : -2]
+        into, out = refs[-2:]
+        loads = [
+            pltpu.make_async_copy(sources[i], held[i], into.at[i]) for i in range(count)
+        ]
+        stores = [
+            pltpu.make_async_copy(held[i], targets[i], out.at[i]) for i in range(count)
+        ]
+        for load in loads:
+            load.start()
+        for load, store in zip(loads, stores):
+            load.wait()
+            store.start()
+        for store in stores:
+            store.wait()
+
+    hbm = pl.BlockSpec(memory_space=pltpu.HBM)
+    return pl.pallas_call(
+        body,
+        out_shape=[jax.ShapeDtypeStruct(a.shape, a.dtype) for a in arrays],
+        in_specs=[hbm] * count,
+        out_specs=[hbm] * count,
+        scratch_shapes=[pltpu.VMEM(a.shape, a.dtype) for a in arrays]
+        + [pltpu.SemaphoreType.DMA((count,)), pltpu.SemaphoreType.DMA((count,))],
+    )(*arrays)
 
 
 def local(
@@ -617,6 +727,7 @@
     b_proj, c_proj, decay_rates, skip_gain, documents,
 ):
     vmem = pl.BlockSpec(memory_space=pltpu.VMEM)
+    hbm = pl.BlockSpec(memory_space=pltpu.HBM)
 
     def out(shape, dtype):
         return jax.ShapeDtypeStruct(shape, dtype)
@@ -625,24 +736,31 @@
         return pltpu.VMEM(shape, F32)
 
     copies = 320
-    wgrad, route, pregrad, ingrad, dgrad, bc, rategrad, skipgrad = pl.pallas_call(
+    arrays = (
+        saved_pre[0].T, w_down.reshape(HID, D), inputs, deltas, mamba_cotangent,
+        b_proj.T, c_proj.T, decay_rates, skip_gain.reshape(1, CH), documents.reshape(1, TOK),
+    )
+    results = [
+        out((HID, D), BF16),
+        out((2, 8), F32),
+        out((HID, 1024), BF16),
+        out((TOK, CH), BF16),
+        out((TOK, CH), BF16),
+        out((NST, TOK), F32),
+        out((NST, TOK), F32),
+        out((NST, CH), F32),
+        out((1, CH), F32),
+    ]
+    wgrad, route, pregrad, ingrad, dgrad, bgrad, cgrad, rategrad, skipgrad = pl.pallas_call(
         kernel,
-        out_shape=(
-            out((HID, D), BF16),
-            out((8, 2), F32),
-            out((NDP, NSEQ, 16, HID), BF16),
-            out((TOK, CH), BF16),
-            out((TOK, CH), BF16),
-            out((8, 8, LANE), F32),
-            out((NST, CH), F32),
-            out((1, CH), F32),
-        ),
-        in_specs=[vmem] * 13,
-        out_specs=[vmem] * 8,
-        scratch_shapes=[
+        out_shape=results,
+        in_specs=[vmem] * 3 + [hbm] * len(arrays),
+        out_specs=[hbm] * len(results),
+        scratch_shapes=[pltpu.VMEM(a.shape, a.dtype) for a in (*arrays, *results)] + [
             pltpu.VMEM((NDP, NSEQ, 16, WIDE), BF16),
             f32(NEX, 2, WIDE), f32(NEX, 2, WIDE), f32(16, WIDE),
-            pltpu.VMEM((HID, 1024), BF16),
+            pltpu.VMEM((HID, 1024), BF16), f32(NDP, NSEQ, 16, HID), f32(HID, 1024),
+            f32(NDP, NSEQ, 16, HID),
             f32(TOK + 8, LANE),
             f32(2, TOK, LANE), f32(2, TOK, LANE), f32(2, TOK, LANE), f32(2, TOK, LANE),
             f32(STEPS, 8, CH), f32(STEPS, 8, CH), f32(STEPS, 8, CH),
@@ -655,28 +773,30 @@
             f32(NST, CH), f32(NST, CH),
             f32(8, 8, LANE), f32(8, 8, LANE), f32(NDP, 8, LANE), f32(8, 8, LANE),
             f32(NST, 2, CH), f32(NSEQ, 2, CH), f32(NST, 1, CH),
-            f32(4, 2, LANE), f32(NSEQ, 2, LANE), f32(NDP, 2, LANE), f32(NEX, 2, LANE),
+            f32(NSEQ, 1, LANE), f32(NSEQ, 1, LANE), f32(NDP, 1, LANE), f32(NEX, 1, LANE),
             pltpu.SemaphoreType.DMA((copies,)),
             pltpu.SemaphoreType.DMA((copies,)),
+            pltpu.SemaphoreType.DMA((len(arrays),)),
+            pltpu.SemaphoreType.DMA((len(results),)),
+            pltpu.SemaphoreType.DMA((8,)),
         ],
         compiler_params=pltpu.CompilerParams(
             collective_id=0, has_side_effects=True, vmem_limit_bytes=56 * 1024 * 1024
         ),
     )(
-        moe_cotangent, route_ids, route_weights,
-        saved_pre.reshape(NDP, NSEQ, 16, HID), w_down.reshape(HID, D),
-        inputs, deltas, mamba_cotangent, b_proj, c_proj, decay_rates,
-        skip_gain.reshape(1, CH), documents.reshape(TOK, 1),
+        moe_cotangent, route_ids.T, route_weights.T, *arrays
     )
-    both = bc.reshape(8, CHUNKS, 2, 2, STEPS).transpose(3, 1, 4, 0, 2).reshape(2, TOK, NST)
+    wgrad, route, pregrad, ingrad, dgrad, bgrad, cgrad, rategrad, skipgrad = hand_over(
+        wgrad, route, pregrad, ingrad, dgrad, bgrad, cgrad, rategrad, skipgrad
+    )
     return (
         wgrad.reshape(1, HID, D),
-        route,
-        pregrad.reshape(1, 1024, HID),
+        route.T,
+        pregrad.T.reshape(1, 1024, HID),
         ingrad,
         dgrad,
-        both[0],
-        both[1],
+        bgrad.T,
+        cgrad.T,
         rategrad,
         skipgrad.reshape(CH),
     )

time: 146 us -> 110 us (0.75)
  local copies, waits for them, and re-layouts: 18.5 us -> 0 us
  Pallas kernels: 126 us -> 109 us
    pallas_call x1 -> x2, Pallas kernels: 126 us -> 109 us  [the longest x1 106 us: local(): pl.pallas_call(kernel, out_shape=results, in_specs=[vmem] * 3 + [hbm] * l...]
    unnamed x22 -> x0, local copies, waits for them, and re-layouts: 14.6 us -> none
    reshape x2 -> x0, local copies, waits for them, and re-layouts: 2.38 us -> none  [the longest x1 1.47 us: local(): documents.reshape(TOK, 1)]
where the time goes in v2:
time: 110 us
  Pallas kernels  109 us (99%)
    pallas_call x1, Pallas kernels, local(): pl.pallas_call(kernel, out_shape=results, in_specs=[vmem] * 3 + [hbm] * l...  106 us
    pallas_call x1, Pallas kernels, hand_over(): pl.pallas_call(body, out_shape=[jax.ShapeDtypeStruct(a.shape, a.dtype) fo...  2.93 us

profile of v2, /device:TPU:1, one launch (start us, length us, event | category | flops | bytes accessed | tf_op | source)
XLA Modules:
  0.0 109.7 jit_solution(10891234502265392055)
XLA Ops:
  0.6 106.1 %shard_map.196 = (bf16[192,4096]{1,0:T(8,128)(2,1)}, f32[2,8]{1,0:T(2,128)}, bf16[192,1024]{1,0:T(8,128)(2,1)}, bf16[256,256]{1,0:T(8,128)(2,1)}, bf16[256,256]{...) custom-call(bf16[8,4096]{1,0:T(8,128)(2,1)} %cot_ref.1, ...), custom_call_target="tpu_custom_call" | custom-call | tf_op jit(solution)/shard_map/pallas_call | solution.py:754
  106.7 2.9 %shard_map.197 = (bf16[192,4096]{1,0:T(8,128)(2,1)}, f32[2,8]{1,0:T(2,128)}, bf16[192,1024]{1,0:T(8,128)(2,1)}, bf16[256,256]{1,0:T(8,128)(2,1)}, bf16[256,256]{...) custom-call(bf16[192,4096]{1,0:T(8,128)(2,1)} %get-tuple-element.27.refs_0_, ...), custom_call_target="tpu_custom_call" | custom-call | tf_op jit(solution)/shard_map/pallas_call | solution.py:715

commit v3 on v2

--- a/solution.py
+++ b/solution.py
@@ -13,11 +13,16 @@
 D, HID, NST, CH, TOK = 4096, 192, 16, 256, 256
 LANE = 128
 WIDE = D + LANE
-CA = 12 * LANE
-CB = CA + 11 * LANE
+CA = 10 * LANE
+CB = CA + 12 * LANE
 CHUNKS, STEPS = 8, TOK // 8
 GROUP = 4
 BIG = 1e9
+ORDER = (
+    "b1", "x1", "p0", "b2", "p1", "y1", "d0", "b3", "x2", "p2", "d1", "b4", "y2", "p3", "d2",
+    "b5", "x3", "b6", "p4", "y3", "d3", "b7", "x4", "p5", "b8", "y4", "d4", "p6", "x5",
+    "y5", "d5", "x6", "p7", "y6", "d6", "x7", "p8", "y7", "d7", "x8", "d8",
+)
 
 
 def get2(ref, rows):
@@ -44,9 +49,9 @@
     ) = near_out
     (
         g, asend, arecv, asm, hid_t, hid_r, slope_t, backs,
-        docs, bc2d, dm2, dx2, ct2, dm, dx, ct, bx, cx, dec, car, g1, g2,
+        docs, bc2d, dm2, dx2, ct2, dm, dx, ct, bx, cx, perm, dec, car, g1, g2,
         ssum, wsum, sin2, win2, summ, gath, ret, back, sbuf, wbuf,
-        bcl, bc1, bc2, bc3, rs, rsr, rgg, rp, rr1, rr2, rr3,
+        bcl, bc1, bc2, bc3, rs, rsr, rgg, rp, rr1, rr3,
         ssem, rsem, isem, osem, tsem,
     ) = refs
     loads = [
@@ -92,6 +97,9 @@
     peers = [{"seq": at_seq(k)} for k in range(1, NSEQ)]
     peers += [{"dp": at_dp(k)} for k in range(1, NDP)]
     peers += [{"expert": at_ex(k)} for k in range(1, NEX)]
+    peers += [
+        {"dp": at_dp(k), "expert": at_ex(j)} for k in range(1, NDP) for j in range(1, NEX)
+    ]
     for peer in peers:
         pl.semaphore_signal(barrier, inc=1, device_id=peer, device_id_type=MESH)
 
@@ -151,8 +159,12 @@
             dx2[h] = d32 * x_ref[:, cols].astype(F32)
             ct2[h] = mc_ref[:, cols].astype(F32)
             for i, ref in enumerate((b_ref, c_ref)):
-                tall = [ref[:, cols], jnp.zeros((LANE - NST, LANE), F32)]
-                bc2d[i, cols, :] = jnp.concatenate(tall, axis=0).T
+                rest, parts = ref[:, cols], []
+                for _ in range(3):
+                    parts.append(rest.astype(BF16).astype(F32))
+                    rest = rest - parts[-1]
+                parts.append(jnp.zeros((LANE - 3 * NST, LANE), F32))
+                bc2d[i, cols, :] = jnp.concatenate(parts, axis=0).T
 
     def spread():
         def body(step, _):
@@ -160,13 +172,25 @@
             dm[step] = get2(dm2, rows)
             dx[step] = get2(dx2, rows)
             ct[step] = get2(ct2, rows)
-            b8, c8 = bc2d[0, rows, :], bc2d[1, rows, :]
-            for n in range(NST):
-                bx[step, n] = jnp.broadcast_to(b8[:, n : n + 1], (8, LANE))
-                cx[step, n] = jnp.broadcast_to(c8[:, n : n + 1], (8, LANE))
+            eight = pl.ds(pl.multiple_of(step * 8, 8), 8)
+            perm[0, eight, :] = bc2d[0, rows, :]
+            perm[1, eight, :] = bc2d[1, rows, :]
             return 0
 
         lax.fori_loop(0, STEPS, body, 0)
+        part = lax.broadcasted_iota(jnp.int32, (LANE, 4 * LANE), 0)
+        lane = lax.broadcasted_iota(jnp.int32, (LANE, 4 * LANE), 1)
+        for quarter in range(NST // 4):
+            state = quarter * 4 + lane // LANE
+            choice = ((part % NST == state) & (part < 3 * NST)).astype(F32).astype(BF16)
+            cols = slice(quarter * 4 * LANE, (quarter + 1) * 4 * LANE)
+            for ref, i in ((bx, 0), (cx, 1)):
+                ref[:, cols] = jnp.dot(
+                    perm[i].astype(BF16), choice, preferred_element_type=F32
+                )
+
+    def spot_of(step, n):
+        return pl.ds(pl.multiple_of(step * 8, 8), 8), slice(n * LANE, (n + 1) * LANE)
 
     def twice(v):
         return jnp.concatenate([v, v], axis=1)
@@ -186,7 +210,7 @@
                 for i, n in enumerate(names):
                     decay = jnp.exp2(d_now * scale[i])
                     dec[n, step] = decay
-                    carry[i] = decay * carry[i] + twice(bx[step, n]) * x_now
+                    carry[i] = decay * carry[i] + twice(bx[spot_of(step, n)]) * x_now
             return tuple(carry)
 
         out = lax.fori_loop(0, STEPS // 2, body, tuple(jnp.zeros((8, CH), F32) for _ in names))
@@ -202,7 +226,7 @@
                 step = STEPS - 1 - (it * 2 + u)
                 c_now = ct[step]
                 for i, n in enumerate(names):
-                    carry[i] = dec[n, step] * (twice(cx[step, n]) * c_now + carry[i])
+                    carry[i] = dec[n, step] * (twice(cx[spot_of(step, n)]) * c_now + carry[i])
             return tuple(carry)
 
         out = lax.fori_loop(0, STEPS // 2, body, tuple(jnp.zeros((8, CH), F32) for _ in names))
@@ -302,7 +326,7 @@
                 for i, n in enumerate(names):
                     carried = dec[n, step] * states[i]
                     car[n, step] = carried
-                    states[i] = carried + twice(bx[step, n]) * x_now
+                    states[i] = carried + twice(bx[spot_of(step, n)]) * x_now
                     total = lanes_sum(states[i] * c_now)
                     sums[i] = jnp.where(here, total, sums[i])
             return tuple(states + sums)
@@ -331,10 +355,10 @@
                 else:
                     sum1, sum2 = get2(g1, rows), get2(g2, rows)
                 for i, n in enumerate(names):
-                    here = twice(cx[step, n]) * c_now + adj[i]
+                    here = twice(cx[spot_of(step, n)]) * c_now + adj[i]
                     adj[i] = dec[n, step] * here
                     product = here * car[n, step]
-                    sum1 = sum1 + twice(bx[step, n]) * here
+                    sum1 = sum1 + twice(bx[spot_of(step, n)]) * here
                     sum2 = sum2 + rates[i] * product
                     grads[i] = grads[i] + d_now * product
                     sums[i] = jnp.where(spot, lanes_sum(here * x_now), sums[i])
@@ -427,9 +451,7 @@
             return g.at[y, seq, :, CA:CB]
         if name == "b2":
             return g.at[y, seq, :, CB:WIDE]
-        if name == "a1":
-            return g.at[0:2, seq, :, 0:CA]
-        return g.at[2:4, seq, :, 0:CA]
+        return g.at[at_dp(int(name)), seq, :, 0:CA]
 
     def gather():
         plus, minus = {"seq": at_seq(1)}, {"seq": at_seq(-1)}
@@ -446,18 +468,18 @@
             arrive(ring_item(name, at_seq(-sign * step)), ring[name, step, sign],
                    minus if sign > 0 else plus)
 
-        across = {}
+        crossing = {}
 
         def across_send(dist):
             seq = at_seq(dist)
-            across[dist] = [channel() for _ in range(4)]
+            crossing[dist] = [channel() for _ in range(4)]
             part = g.at[y, seq, :, CA:WIDE]
-            start(part, part, across[dist][0], up)
-            start(part, part, across[dist][1], down)
+            start(part, part, crossing[dist][0], up)
+            start(part, part, crossing[dist][1], down)
 
         def across_pass(dist):
             seq = at_seq(dist)
-            slots = across[dist]
+            slots = crossing[dist]
             arrive(g.at[at_dp(-1), seq, :, CA:WIDE], slots[0], down)
             half = g.at[at_dp(-1), seq, :, CA:CB]
             start(half, half, slots[2], up)
@@ -467,7 +489,7 @@
 
         def across_end(dist):
             seq = at_seq(dist)
-            slots = across[dist]
+            slots = crossing[dist]
             arrive(g.at[at_dp(2), seq, :, CA:CB], slots[2], down)
             arrive(g.at[at_dp(2), seq, :, CB:WIDE], slots[3], up)
 
@@ -478,55 +500,67 @@
         ring_send("b", 1, 1)
         ring_send("b", 1, -1)
         across_send(0)
+        ring_send("0", 1, 1)
+        ring_send("0", 1, -1)
         yield
         for k in range(1, NDP):
             arrive(g.at[at_dp(-k), z, :, 0:CA], first[k - 1], {"dp": at_dp(-k)})
-        for name in ("a1", "a2"):
+        for name in "123":
             ring_send(name, 1, 1)
             ring_send(name, 1, -1)
         yield
         half = NSEQ // 2
-        pending, passed = [0], []
-        for step in range(1, half):
-            for name in ("b", "a1", "a2"):
+
+        def both(step):
+            return {0: [0], half: [half]}.get(step, [-step, step])
+
+        def ring_b(step):
+            if step == half:
+                ring_wait("b1", half, 1)
+                ring_wait("b2", half, -1)
+            else:
                 for sign in (1, -1):
+                    ring_wait("b", step, sign)
+                    if step < half - 1:
+                        ring_send("b", step + 1, sign)
+                    else:
+                        ring_send("b1" if sign > 0 else "b2", half, sign)
+            for dist in both(step):
+                across_send(dist)
+
+        def ring_a(name, step):
+            for sign in (1, -1):
+                near = (name in "01") == (sign > 0)
+                if step < half or near:
                     ring_wait(name, step, sign)
-                    if step < half - 1:
-                        ring_send(name, step + 1, sign)
-                    elif name == "b":
-                        ring_send("b1" if sign > 0 else "b2", half, sign)
-                    elif (name == "a1") == (sign > 0):
-                        ring_send(name, half, sign)
-                if name == "b":
-                    across_send(-step)
-                    across_send(step)
-                elif name == "a1":
-                    for dist in pending:
-                        across_pass(dist)
-                else:
-                    for dist in passed:
-                        across_end(dist)
-                    seq_block(passed)
-                    pending, passed = [-step, step], pending
+                if step < half - 1 or (step == half - 1 and near):
+                    ring_send(name, step + 1, sign)
+
+        def across(step):
+            for dist in both(step):
+                across_pass(dist)
+
+        def done(step):
+            for dist in both(step):
+                across_end(dist)
+            seq_block(both(step))
+
+        for turn in ORDER:
+            kind, step = turn[:-1], int(turn[-1])
+            if kind == "b":
+                ring_b(step)
                 yield
-        ring_wait("b1", half, 1)
-        ring_wait("b2", half, -1)
-        across_send(half)
-        yield
-        for dist in pending:
-            across_pass(dist)
-        for dist in passed:
-            across_end(dist)
-        seq_block(passed)
-        yield
-        across_pass(half)
-        ring_wait("a1", half, 1)
-        ring_wait("a2", half, -1)
-        for dist in pending:
-            across_end(dist)
-        seq_block(pending)
-        across_end(half)
-        seq_block([half])
+            elif kind == "p":
+                across(step)
+            elif kind == "d":
+                done(step)
+            else:
+                for name in {"x": "01", "y": "23"}[kind]:
+                    ring_a(name, step)
+                if step == half:
+                    for name in "23":
+                        ring_a(name, step)
+                yield
 
     def hidden_block(block):
         cols = slice(block * 256, (block + 1) * 256)
@@ -574,10 +608,9 @@
     def weight_tile(tile, _):
         width = 512
         cols = pl.ds(pl.multiple_of(tile * width, width), width)
-        scale = g[:, :, :, D:WIDE].reshape(1024, LANE).astype(F32)
+        scale = g[:, :, :, D:WIDE].reshape(1024, LANE)
         scale = jnp.concatenate([scale] * (width // LANE), axis=1)
-        rows = g[:, :, :, cols].reshape(1024, width).astype(F32)
-        scaled = (rows * scale).astype(BF16)
+        scaled = g[:, :, :, cols].reshape(1024, width) * scale
         wgrad_ref[:, cols] = jnp.dot(
             hid_t[...], scaled, preferred_element_type=F32
         ).astype(BF16)
@@ -653,21 +686,21 @@
     total = rr1[0]
     for p in range(1, NSEQ):
         total = total + rr1[p]
-    rr2[y] = total
-    by_dp = [channel() for _ in range(1, NDP)]
-    for k in range(1, NDP):
-        start(rr2.at[y], rr2.at[y], by_dp[k - 1], {"dp": at_dp(k)})
+    rr3[y * NEX + e] = total
+    others = [(k, j) for k in range(NDP) for j in range(NEX) if (k, j) != (0, 0)]
+    last = {pair: channel() for pair in others}
+    for k, j in others:
+        start(rr3.at[y * NEX + e], rr3.at[y * NEX + e], last[k, j],
+              {"dp": at_dp(k), "expert": at_ex(j)})
     slopes()
     stores[2].start()
-    for k in range(1, NDP):
-        arrive(rr2.at[at_dp(-k)], by_dp[k - 1], {"dp": at_dp(-k)})
-    rr3[e] = ((rr2[0] + rr2[1]) + rr2[2]) + rr2[3]
-    by_ex = [channel() for _ in range(1, NEX)]
-    for k in range(1, NEX):
-        start(rr3.at[e], rr3.at[e], by_ex[k - 1], {"expert": at_ex(k)})
     lax.fori_loop(4, 8, weight_tile, 0)
-    for k in range(1, NEX):
-        arrive(rr3.at[at_ex(-k)], by_ex[k - 1], {"expert": at_ex(-k)})
+    for k, j in others:
+        arrive(rr3.at[at_dp(-k) * NEX + at_ex(-j)], last[k, j],
+               {"dp": at_dp(-k), "expert": at_ex(-j)})
+    tables = [
+        ((rr3[x] + rr3[NEX + x]) + rr3[2 * NEX + x]) + rr3[3 * NEX + x] for x in range(NEX)
+    ]
 
     base = y * 16 + e * 2
     picked = jnp.zeros((8, LANE), F32)
@@ -675,7 +708,7 @@
         values = jnp.zeros((1, LANE), F32)
         for x in range(NEX):
             here = lane8[0:1, :] == base + c
-            value = jnp.sum(jnp.where(here, rr3[x], 0.0), axis=1, keepdims=True)
+            value = jnp.sum(jnp.where(here, tables[x], 0.0), axis=1, keepdims=True)
             values = jnp.where(lane8[0:1, :] == x, value, values)
         picked = picked + slot_of[c] * values
     for k, names in enumerate((named_first, named_second)):
@@ -764,7 +797,7 @@
             f32(TOK + 8, LANE),
             f32(2, TOK, LANE), f32(2, TOK, LANE), f32(2, TOK, LANE), f32(2, TOK, LANE),
             f32(STEPS, 8, CH), f32(STEPS, 8, CH), f32(STEPS, 8, CH),
-            f32(STEPS, NST, 8, LANE), f32(STEPS, NST, 8, LANE),
+            f32(TOK, NST * LANE), f32(TOK, NST * LANE), f32(2, TOK, LANE),
             f32(NST, STEPS, 8, CH), f32(NST, STEPS, 8, CH),
             f32(2, TOK, LANE), f32(2, TOK, LANE),
             f32(2, TOK // 2, LANE), f32(2, TOK // 2, LANE),
@@ -773,7 +806,7 @@
             f32(NST, CH), f32(NST, CH),
             f32(8, 8, LANE), f32(8, 8, LANE), f32(NDP, 8, LANE), f32(8, 8, LANE),
             f32(NST, 2, CH), f32(NSEQ, 2, CH), f32(NST, 1, CH),
-            f32(NSEQ, 1, LANE), f32(NSEQ, 1, LANE), f32(NDP, 1, LANE), f32(NEX, 1, LANE),
+            f32(NSEQ, 1, LANE), f32(NSEQ, 1, LANE), f32(NDP * NEX, 1, LANE),
             pltpu.SemaphoreType.DMA((copies,)),
             pltpu.SemaphoreType.DMA((copies,)),
             pltpu.SemaphoreType.DMA((len(arrays),)),

time: 110 us -> 106 us (0.964)
  Pallas kernels: 109 us -> 106 us
    pallas_call x1, Pallas kernels: 106 us -> 103 us  [local(): pl.pallas_call(kernel, out_shape=results, in_specs=[vmem] * 3 + [hbm] * l...]
where the time goes in v3:
time: 106 us
  Pallas kernels  106 us (100%)
    pallas_call x1, Pallas kernels, local(): pl.pallas_call(kernel, out_shape=results, in_specs=[vmem] * 3 + [hbm] * l...  103 us
    pallas_call x1, Pallas kernels, hand_over(): pl.pallas_call(body, out_shape=[jax.ShapeDtypeStruct(a.shape, a.dtype) fo...  2.93 us

profile of v3, /device:TPU:1, one launch (start us, length us, event | category | flops | bytes accessed | tf_op | source)
XLA Modules:
  0.0 106.2 jit_solution(16801800540439108516)
XLA Ops:
  0.6 102.6 %shard_map.196 = (bf16[192,4096]{1,0:T(8,128)(2,1)}, f32[2,8]{1,0:T(2,128)}, bf16[192,1024]{1,0:T(8,128)(2,1)}, bf16[256,256]{1,0:T(8,128)(2,1)}, bf16[256,256]{...) custom-call(bf16[8,4096]{1,0:T(8,128)(2,1)} %cot_ref.1, ...), custom_call_target="tpu_custom_call" | custom-call | tf_op jit(solution)/shard_map/pallas_call | solution.py:787
  103.2 2.9 %shard_map.197 = (bf16[192,4096]{1,0:T(8,128)(2,1)}, f32[2,8]{1,0:T(2,128)}, bf16[192,1024]{1,0:T(8,128)(2,1)}, bf16[256,256]{1,0:T(8,128)(2,1)}, bf16[256,256]{...) custom-call(bf16[192,4096]{1,0:T(8,128)(2,1)} %get-tuple-element.27.refs_0_, ...), custom_call_target="tpu_custom_call" | custom-call | tf_op jit(solution)/shard_map/pallas_call | solution.py:748
